TPU v7x, 512 devices: a whole 4x4x16 slice. The times are simulated.
512 devices in a mesh: dp: 64 (over x_lo, z, core), blk: 8 (over x_hi, y).
Axes of the slice: x: 4 (x_hi: 2, x_lo: 2; x = x_hi * 2 + x_lo), y: 4, z: 16, core: 2. Of those that a mesh axis runs over, the one named last changes fastest.
Arguments:
- pooled_grad: bfloat16 [32768, 64, 256], P(('dp', 'blk')), may hold values from -6 to 6
- bag_ids: int32 [64, 64, 8, 64, 4], P('dp', None, 'blk'), may hold values from 0 to 1023
- bag_lengths: int32 [64, 64, 8, 64], P('dp', None, 'blk'), may hold values from 1 to 4
- slot_table: int32 [64], replicated, may hold values from 0 to 63, each once
- layer_input: bfloat16 [32768, 128], P(('dp', 'blk')), may hold values from -100 to 100
- layer_grad_out: bfloat16 [32768, 4096], P(('dp', 'blk')), may hold values from -1 to 1
- left_stats: float32 [32, 1, 128, 128], P('blk', None, 'dp'), may hold values from -600 to 600
- right_stats: float32 [32, 1, 128, 128], P('blk', None, 'dp'), may hold values from -600 to 600
- left_root: float32 [32, 1, 128, 128], P('blk'), may hold values from -3 to 3
- right_root: float32 [32, 1, 128, 128], P('blk'), may hold values from -3 to 3
- second_moment: float32 [1, 128, 4096], P(None, None, 'blk'), may hold values from 0.01 to 10
Outputs:
- table_grad: float32 [64, 1024, 256], P('dp', 'blk')
- left_new: float32 [32, 1, 128, 128], P('blk', None, 'dp')
- right_new: float32 [32, 1, 128, 128], P('blk', None, 'dp')
- moment_new: float32 [1, 128, 4096], P(None, 'dp', 'blk')
- update: bfloat16 [1, 128, 4096], replicated
All inputs are finite; a program needn't handle non-finite values.
Results may differ from a plain program's by a relative error of at most 0.001.
Values may be sent and summed in bfloat16 or wider, within the bound.
A program may use at most 128 MiB of HBM per device.

v0:
```python
import jax
import jax.numpy as jnp
from jax import lax
from jax.sharding import PartitionSpec as P

ROWS_DEV = 128


second_beta = 0.9
graft_epsilon = 1e-08
norm_epsilon = 1e-06
highest = lax.Precision.HIGHEST


def per_device(
    pooled_grad,
    bag_ids,
    bag_lengths,
    slot_table,
    layer_input,
    layer_grad_out,
    left_stats,
    right_stats,
    left_root,
    right_root,
    second_moment,
):
    block_size = left_root.shape[2]
    block_rows = left_root.shape[1]
    owned_cols = left_root.shape[0]
    owned_width = owned_cols * block_size
    dp_index = lax.axis_index("dp")
    share = block_size // lax.axis_size("dp")
    tables_here = bag_ids.shape[0]
    pool_size = bag_ids.shape[-1]
    table_rows = ROWS_DEV * lax.axis_size("blk")
    id_lists = bag_ids.reshape(tables_here, -1, pool_size)
    length_values = bag_lengths.reshape(tables_here, -1)
    inverse = 1.0 / length_values.astype(jnp.float32)
    weights = [jnp.where(position < length_values, inverse, 0.0) for position in range(pool_size)]
    ordered = jnp.take(pooled_grad, slot_table, axis=1)
    received = lax.all_to_all(ordered, "dp", split_axis=1, concat_axis=0, tiled=True)
    column = received[:, 0, :].astype(jnp.float32)
    accumulator = jnp.zeros((table_rows, received.shape[2]), jnp.float32)
    for position in range(pool_size):
        accumulator = accumulator.at[id_lists[0, :, position]].add(
            column * weights[position][0][:, None]
        )
    outputs = [accumulator]
    dense = jnp.stack(outputs)
    table_grad = lax.psum_scatter(dense, "blk", scatter_dimension=1, tiled=True)
    partial_grad = lax.dot_general(
        layer_input, layer_grad_out, (((0,), (0,)), ((), ())), preferred_element_type=jnp.float32
    )
    total = lax.psum(partial_grad, ("dp", "blk"))
    owned = lax.dynamic_slice_in_dim(total, lax.axis_index("blk") * owned_width, owned_width, 1)
    blocks = jnp.transpose(
        owned.reshape(block_rows, block_size, owned_cols, block_size), (2, 0, 1, 3)
    )
    my_rows = lax.dynamic_slice_in_dim(blocks, dp_index * share, share, 2)
    my_columns = lax.dynamic_slice_in_dim(blocks, dp_index * share, share, 3)
    left_new = left_stats + jnp.einsum("crij,crkj->crik", my_rows, blocks, precision=highest)
    right_new = right_stats + jnp.einsum("crji,crjk->crik", my_columns, blocks, precision=highest)
    grad_rows = jnp.transpose(blocks, (1, 2, 0, 3)).reshape(block_rows, block_size, owned_width)
    moment_full = second_beta * second_moment + (1.0 - second_beta) * grad_rows * grad_rows
    moment_new = lax.dynamic_slice_in_dim(moment_full, dp_index * share, share, 1)
    graft_rows = grad_rows / (jnp.sqrt(moment_full) + graft_epsilon)
    graft = jnp.transpose(
        graft_rows.reshape(block_rows, block_size, owned_cols, block_size), (2, 0, 1, 3)
    )
    left_part = lax.dynamic_slice_in_dim(left_root, dp_index * share, share, 2)
    halfway = jnp.einsum("crij,crjk->crik", left_part, blocks, precision=highest)
    precond = jnp.einsum("crij,crjk->crik", halfway, right_root, precision=highest)
    graft_part = lax.dynamic_slice_in_dim(graft, dp_index * share, share, 2)
    graft_square, precond_square = lax.psum(
        (jnp.sum(graft_part * graft_part, axis=(2, 3)), jnp.sum(precond * precond, axis=(2, 3))),
        "dp",
    )
    ratio = jnp.sqrt(graft_square / (precond_square + norm_epsilon))
    part_update = (precond * ratio[:, :, None, None]).astype(jnp.bfloat16)
    part_rows = jnp.transpose(part_update, (1, 2, 0, 3)).reshape(block_rows, share, owned_width)
    local_update = lax.all_gather(part_rows, "dp", axis=1, tiled=True)
    update = lax.all_gather(local_update, "blk", axis=2, tiled=True)
    return (table_grad, left_new, right_new, moment_new, update)


def solution(mesh):
    placed = (
        P(("dp", "blk"), None, None),
        P("dp", None, "blk", None, None),
        P("dp", None, "blk", None),
        P(),
        P(("dp", "blk"), None),
        P(("dp", "blk"), None),
        P("blk", None, "dp", None),
        P("blk", None, "dp", None),
        P("blk", None, None, None),
        P("blk", None, None, None),
        P(None, None, "blk"),
    )
    return jax.shard_map(
        per_device,
        mesh=mesh,
        in_specs=placed,
        out_specs=(
            P("dp", "blk", None),
            P("blk", None, "dp", None),
            P("blk", None, "dp", None),
            P(None, "dp", "blk"),
            P(),
        ),
        check_vma=False,
    )
```

profile of v0, /device:TPU:24, one launch (start us, length us, event | category | flops | bytes accessed | tf_op | source)
XLA Modules:
  0.0 910.4 jit_solution(674711418423465086)
XLA Ops:
  7.2 0.8 compare_select_fusion.8
  8.0 0.7 compare_and_fusion
  8.7 0.1 copy-done
  8.8 7.9 gather_fusion
  16.7 1.8 select_bitcast_fusion
  18.6 2.5 copy.50
  21.1 17.4 %all-to-all-start = ((bf16[64,64,256]{2,0,1:T(8,128)(2,1)}), bf16[64,64,256]{2,0,1:T(8,128)(2,1)}, u32[]{:S(2)}, u32[]{:S(2)}) async-start(bf16[64,64,256]{2,0,1:T(8,128)(2,1)} %copy.50), calls=%async_computation | async-start | bytes 4194304 | tf_op jit(solution)/shard_map/all_to_all | solution.py:42
  38.6 1.8 fusion.28
  40.6 0.4 fusion.17
  41.3 505.9 %all-reduce.3.cloned.1.call-done = f32[128,4096]{1,0:T(8,128)} async-done(((f32[128,4096]{1,0:T(8,128)}), f32[128,4096]{1,0:T(8,128)}) %all-reduce.3.cloned.1.call-update) | async-done | bytes 2097168 | tf_op jit(solution)/shard_map/psum | solution.py:55
  547.2 1.1 bitcast_divide_fusion
  548.3 0.1 copy.51
  548.4 0.1 copy.52
  548.6 0.1 multiply_reduce_fusion.1
  548.8 1.0 fusion.10
  549.8 1.4 multiply_reduce_fusion
  551.2 106.0 %all-reduce = (f32[4,1]{0,1:T(1,128)S(1)}, f32[4,1]{0,1:T(1,128)S(1)}) all-reduce(f32[4,1]{0,1:T(1,128)S(1)} %bitcast.117, f32[4,1]{0,1:T(1,128)S(1)} %bitcast.116), channel_id=1, replica_groups=mesh['dp'=64,'blk'=8] {'dp'}, use_global_device_ids=true, to_apply=%region_7.8 | all-reduce | flops 8 | bytes 64 | tf_op jit(solution)/shard_map/psum | solution.py:75
  657.3 65.2 %all_gather.6 = bf16[1,128,512]{2,0,1:T(2,128)(2,1)} all-gather(bf16[1,2,512]{2,0,1:T(2,128)(2,1)S(1)} %copy.56), channel_id=1, replica_groups=mesh['dp'=64,'blk'=8] {'dp'}, dimensions={1}, use_global_device_ids=true | all-gather | bytes 133120 | tf_op jit(solution)/shard_map/all_gather | solution.py:82
  722.5 0.2 reduce-scatter.2.cloned.1.call-start
  722.7 0.7 compare_select_fusion.4
  723.4 7.5 bitcast_multiply_fusion
  731.0 23.1 %scatter_custom_fusion = f32[1024,256]{1,0:T(8,128)S(1)} fusion(s32[4096]{0:T(1024)} %bitcast.115, f32[4096,256]{1,0:T(8,128)} %get-tuple-element.41, f32[]{:T(128)} %constant.20.clone.1), kind=kCustom, calls=%fused_computation.16 | custom fusion | flops 1048576 | bytes 1049088 | tf_op jit(solution)/shard_map/scatter-add | solution.py:46
  754.1 23.3 %scatter_fusion = f32[1024,256]{1,0:T(8,128)S(1)} fusion(f32[1024,256]{1,0:T(8,128)S(1)} %scatter_custom_fusion, s32[4096]{0:T(1024)S(1)} %bitcast.114, f32[4096,256]{1,0:T(8,128)} %get-tuple-element.39), kind=kCustom, calls=%fused_computation.2 | custom fusion | flops 1048576 | bytes 12599296 | tf_op jit(solution)/shard_map/scatter-add | solution.py:46
  777.4 23.3 %scatter_fusion.1 = f32[1024,256]{1,0:T(8,128)S(1)} fusion(f32[1024,256]{1,0:T(8,128)S(1)} %scatter_fusion, s32[4096]{0:T(1024)S(1)} %bitcast.113, f32[4096,256]{1,0:T(8,128)} %get-tuple-element.40), kind=kCustom, calls=%fused_computation.3 | custom fusion | flops 1048576 | bytes 12599296 | tf_op jit(solution)/shard_map/scatter-add | solution.py:46
  800.7 23.3 %scatter_fusion.2 = f32[1024,256]{1,0:T(8,128)S(1)} fusion(f32[1024,256]{1,0:T(8,128)S(1)} %scatter_fusion.1, s32[4096]{0:T(1024)S(1)} %bitcast.112, f32[4096,256]{1,0:T(8,128)} %get-tuple-element.38), kind=kCustom, calls=%fused_computation.4 | custom fusion | flops 1048576 | bytes 12599296 | tf_op jit(solution)/shard_map/scatter-add | solution.py:46
  824.0 1.0 copy-done.1
  825.0 1.1 fusion.7
  826.0 0.6 constant_dynamic-slice_fusion
  826.7 1.1 fusion.3
  827.8 1.6 fusion.1
  829.4 3.7 copy.59
  833.1 70.8 %reduce-scatter.2.cloned.1.call-done = f32[1,128,256]{2,1,0:T(8,128)} async-done(((f32[1,1024,256]{2,1,0:T(8,128)}), f32[1,128,256]{2,1,0:T(8,128)}) %reduce-scatter.2.cloned.1.call-update) | async-done | bytes 131088 | tf_op jit(solution)/shard_map/reduce_scatter | solution.py:51
  (42 shorter events, 0.8 us)
Async XLA Ops:
  7.2 1.6 copy-start
  18.5 20.1 %copy-start.5 = (bf16[64,4096]{1,0:T(8,128)(2,1)S(1)}, bf16[64,4096]{1,0:T(8,128)(2,1)}, u32[]{:S(2)}) copy-start(bf16[64,4096]{1,0:T(8,128)(2,1)} %param.16) | copy-start | bytes 1572868
  18.5 20.1 %copy-start.10 = (bf16[64,128]{1,0:T(8,128)(2,1)S(1)}, bf16[64,128]{1,0:T(8,128)(2,1)}, u32[]{:S(2)}) copy-start(bf16[64,128]{1,0:T(8,128)(2,1)} %param.15) | copy-start | bytes 49156
  21.1 19.4 %copy-start.6 = (s32[1,64,1,64,4]{3,4,2,1,0:T(4,128)S(1)}, s32[1,64,1,64,4]{3,4,2,1,0:T(4,128)}, u32[]{:S(2)}) copy-start(s32[1,64,1,64,4]{3,4,2,1,0:T(4,128)} %param.12) | copy-start | bytes 196612
  21.1 19.5 %copy-start.9 = (s32[1,64,1,64]{3,2,1,0:T(1,128)S(1)}, s32[1,64,1,64]{3,2,1,0:T(1,128)}, u32[]{:S(2)}) copy-start(s32[1,64,1,64]{3,2,1,0:T(1,128)} %param.13) | copy-start | bytes 49156
  21.1 526.1 %copy-start.4 = (f32[1,128,512]{2,1,0:T(8,128)S(1)}, f32[1,128,512]{2,1,0:T(8,128)}, u32[]{:S(2)}) copy-start(f32[1,128,512]{2,1,0:T(8,128)} %param.21) | copy-start | bytes 786436
  21.1 702.3 %all-to-all-start = ((bf16[64,64,256]{2,0,1:T(8,128)(2,1)}), bf16[64,64,256]{2,0,1:T(8,128)(2,1)}, u32[]{:S(2)}, u32[]{:S(2)}) async-start(bf16[64,64,256]{2,0,1:T(8,128)(2,1)} %copy.50), calls=%async_computation | async-start | bytes 4194304 | tf_op jit(solution)/shard_map/all_to_all | solution.py:42
  38.5 508.6 %all-reduce.3.cloned.1.call-start = ((), (), s32[]{:S(2)}) async-start(), calls=%async_computation.3 | async-start | bytes 4194304 | tf_op jit(solution)/shard_map/psum | solution.py:55
  40.4 789.0 %all-gather.2.cloned.1.call-start = ((), (), s32[]{:S(2)}) async-start(), calls=%async_computation.4 | async-start | bytes 2359296 | tf_op jit(solution)/shard_map/all_gather | solution.py:83
  548.3 182.7 %copy-start.2 = (f32[128,512]{1,0:T(8,128)}, f32[128,512]{1,0:T(8,128)S(1)}, u32[]{:S(2)}) copy-start(f32[128,512]{1,0:T(8,128)S(1)} %get-tuple-element.37) | copy-start | bytes 786436
  548.4 182.6 %copy-start.3 = (f32[128,512]{0,1:T(8,128)}, f32[128,512]{0,1:T(8,128)S(1)}, u32[]{:S(2)}) copy-start(f32[128,512]{0,1:T(8,128)S(1)} %copy.51) | copy-start | bytes 786436
  722.5 181.4 %reduce-scatter.2.cloned.1.call-start = ((), (), s32[]{:S(2)}) async-start(), calls=%async_computation.2 | async-start | bytes 1179648 | tf_op jit(solution)/shard_map/reduce_scatter | solution.py:51
  723.4 30.7 %copy-start.8 = (s32[4096,1]{0,1:T(1,128)S(1)}, s32[4096,1]{0,1:T(1,128)}, u32[]{:S(2)}) copy-start(s32[4096,1]{0,1:T(1,128)} %get-tuple-element.44) | copy-start | bytes 49156
  754.1 23.3 %copy-start.7 = (s32[4096,1]{0,1:T(1,128)S(1)}, s32[4096,1]{0,1:T(1,128)}, u32[]{:S(2)}) copy-start(s32[4096,1]{0,1:T(1,128)} %get-tuple-element.43) | copy-start | bytes 49156
  800.7 26.0 %copy-start.11 = (f32[4,1,2,128]{3,2,1,0:T(2,128)S(1)}, f32[4,1,2,128]{3,2,1,0:T(2,128)}, u32[]{:S(2)}) copy-start(f32[4,1,2,128]{3,2,1,0:T(2,128)} %param.17) | copy-start | bytes 12292
  800.7 27.1 %copy-start.12 = (f32[4,1,2,128]{3,2,1,0:T(2,128)S(1)}, f32[4,1,2,128]{3,2,1,0:T(2,128)}, u32[]{:S(2)}) copy-start(f32[4,1,2,128]{3,2,1,0:T(2,128)} %param.18) | copy-start | bytes 12292
  823.9 1.0 copy-start.1
Sparse Core Ops, SparseCore 0:
  44.7 502.3 all-reduce.2
  722.6 59.8 all-gather.1
  825.1 78.7 reduce-scatter.1
where the time goes:
time: 911 us; the launch traced here: 910 us
  waiting for transfers between devices  577 us (63%)
  blocking collectives  171 us (19%)
  other arithmetic  107 us (12%)
  starting transfers between devices  17.7 us (2%)
  local copies, waits for them, and re-layouts  16.7 us (2%)
  between operations  14 us (2%)
    psum x1, waiting for transfers between devices, per_device(): total = lax.psum(partial_grad, ('dp', 'blk'))  506 us
    psum x1, blocking collectives, per_device(): lax.psum((jnp.sum(graft_part * graft_part, axis=(2, 3)), jnp.sum(precond...  106 us
    scatter-add x4, other arithmetic, per_device(): accumulator.at[id_lists[0, :, position]]  92.9 us
    reduce_scatter x1, waiting for transfers between devices, per_device(): table_grad = lax.psum_scatter(dense, 'blk', scatter_dimension=1, tiled=True)  70.8 us
    all_gather x1, blocking collectives, per_device(): local_update = lax.all_gather(part_rows, 'dp', axis=1, tiled=True)  65.2 us
  transfers between devices with their start and end apart: 4, of which 2 were waited for; matrix products, arithmetic and copies ran while one was open for 13% of the time, Pallas kernels for 0%

commit v1 on v0

v1 whole, which is shorter than its diff:
```python
import functools

import jax
import jax.numpy as jnp
from jax import lax
from jax.experimental import pallas as pl
from jax.experimental.pallas import tpu as pltpu
from jax.sharding import PartitionSpec as P

MESH = pl.DeviceIdType.MESH
F32, BF16 = jnp.float32, jnp.bfloat16
CORES, XLO = 2, 2
GROUP = CORES * XLO
POOL = 4
HALVES = 2

second_beta = 0.9
graft_epsilon = 1e-08
norm_epsilon = 1e-06
highest = lax.Precision.HIGHEST


def arrange_kernel(depth, columns, slots_ref, x_ref, ids_ref, len_ref, raw_ref, out_ids_ref, wide):
    samples, tables, edim = x_ref.shape
    width = edim // HALVES
    shares = depth // columns

    def widen(s, carry):
        rows = pl.ds(pl.multiple_of(s * tables, tables), tables)
        for h in range(HALVES):
            wide[h, rows, :] = x_ref[s, :, h * width : (h + 1) * width].astype(F32)
        return carry

    lax.fori_loop(0, samples, widen, 0)

    def pick(q, carry):
        col, g = q // GROUP, q % GROUP
        for i in range(shares):
            slot = ((g // CORES) * depth + col * shares + i) * CORES + g % CORES
            table = slots_ref[slot]
            for h in range(HALVES):
                rows = wide[h, pl.ds(table, samples, stride=tables), :]
                raw_ref[h, q, i] = rows.astype(BF16)
        return carry

    lax.fori_loop(0, columns * GROUP, pick, 0)
    position = lax.broadcasted_iota(jnp.int32, (POOL, samples), 0)

    def mask(z, carry):
        for xl in range(XLO):
            for core in range(CORES):
                source = (xl * depth + z) * CORES + core
                bag = len_ref[pl.ds(source, 1), :]
                kept = jnp.where(position < bag, ids_ref[source], -1)
                out_ids_ref[z, xl * POOL : (xl + 1) * POOL, core * samples : (core + 1) * samples] = kept
        return carry

    lax.fori_loop(0, depth, mask, 0)


def main_kernel(
    depth,
    columns,
    raw_ref,
    ids_ref,
    x_ref,
    y_ref,
    left_stats_ref,
    right_stats_ref,
    left_root_ref,
    right_root_ref,
    moment_ref,
    table_ref,
    left_ref,
    right_ref,
    moment_new_ref,
    update_ref,
    idr,
    onehot,
    raw,
    up,
    down,
    final,
    xr,
    yr,
    part,
    parts,
    own_sum,
    grad,
    lmat,
    rmat,
    mmat,
    stage,
    stats,
    block_update,
    ids_sem,
    raw_sem,
    dense_sem,
    up_sem,
    down_sem,
    table_sem,
    parts_sem,
    grad_sem,
    stats_sem,
    update_sem,
    send_sem,
):
    plane = columns * GROUP
    shares = depth // columns
    half = depth // 2
    bs = lmat.shape[0]
    share = left_ref.shape[2]
    dp, blk = lax.axis_index("dp"), lax.axis_index("blk")
    core = dp % CORES
    z = (dp // CORES) % depth
    xl = dp // (CORES * depth)
    g = xl * CORES + core
    me = blk * GROUP + g

    def dp_of(xl_of, z_of, core_of):
        return (xl_of * depth + z_of) * CORES + core_of

    def in_plane(q):
        other = q % GROUP
        return (dp_of(other // CORES, z, other % CORES), q // GROUP)

    def along_z(z_of):
        return (dp_of(xl, z_of, core), blk)

    def loop(first, last, body):
        def step(k, carry):
            body(k)
            return carry

        lax.fori_loop(first, last, step, 0)

    def remote(src, dst, sent, arrived, device):
        return pltpu.make_async_remote_copy(
            src_ref=src, dst_ref=dst, send_sem=sent, recv_sem=arrived, device_id=device, device_id_type=MESH
        )

    def drain(ref, sem):
        pltpu.make_async_copy(ref, ref, sem).wait()

    ids_self = blk == z // shares
    piece_z = blk * shares + z // columns
    piece_blk = z % columns
    piece_self = jnp.logical_and(piece_z == z, piece_blk == blk)
    from_z = (z % shares) * columns + blk
    from_blk = z // shares

    barrier = pltpu.get_barrier_semaphore()

    def greet(device):
        pl.semaphore_signal(barrier, inc=1, device_id=device, device_id_type=MESH)

    loop(1, plane, lambda o: greet(in_plane((me + o) % plane)))
    loop(1, depth, lambda o: greet(along_z((z + o) % depth)))

    def greet_ids(k):
        z_of, blk_of = blk * shares + k // columns, k % columns

        @pl.when(jnp.logical_not(jnp.logical_and(z_of == z, blk_of == blk)))
        def _():
            greet((dp_of(xl, z_of, core), blk_of))

    loop(0, depth, greet_ids)

    @pl.when(jnp.logical_not(piece_self))
    def _():
        greet((dp_of(xl, from_z, core), from_blk))

    greetings = (plane - 1) + (depth - 1) + depth + 1
    pl.semaphore_wait(barrier, greetings - ids_self.astype(jnp.int32) - piece_self.astype(jnp.int32))

    def send_ids(k):
        z_of = (z + k) % depth
        itself = jnp.logical_and(z_of == z, ids_self)
        place = idr.at[z % shares, blk]

        @pl.when(itself)
        def _():
            pltpu.make_async_copy(ids_ref.at[z_of], place, ids_sem).start()

        @pl.when(jnp.logical_not(itself))
        def _():
            remote(ids_ref.at[z_of], place, send_sem.at[0], ids_sem, (dp_of(xl, z_of, core), z // shares)).start()

    loop(0, depth, send_ids)

    def send_raw(h):
        pltpu.make_async_copy(raw_ref.at[h, me], raw.at[h, me], raw_sem.at[h]).start()

        def one(o):
            q = (me + o) % plane
            remote(raw_ref.at[h, q], raw.at[h, me], send_sem.at[1], raw_sem.at[h], in_plane(q)).start()

        loop(1, plane, one)

    def send_dense():
        def y_part(q):
            return y_ref.at[:, pl.ds(pl.multiple_of(q * bs, bs), bs)]

        pltpu.make_async_copy(x_ref, xr.at[me], dense_sem.at[0]).start()
        pltpu.make_async_copy(y_part(me), yr.at[me], dense_sem.at[1]).start()

        def one(o):
            q = (me + o) % plane
            remote(x_ref, xr.at[me], send_sem.at[2], dense_sem.at[0], in_plane(q)).start()
            remote(y_part(q), yr.at[me], send_sem.at[3], dense_sem.at[1], in_plane(q)).start()

        loop(1, plane, one)

    send_raw(0)
    send_dense()
    send_raw(1)

    drain(idr, ids_sem)
    rows = lax.broadcasted_iota(jnp.int32, (bs, 128), 0)

    def weigh(k):
        i, source = k // columns, k % columns
        tile = idr[i, source]
        for x_of in range(XLO):
            ids = [tile[x_of * POOL + p : x_of * POOL + p + 1, :] for p in range(POOL)]
            length = sum((one >= 0).astype(jnp.int32) for one in ids)
            value = jnp.where(length == 1, 12.0, jnp.where(length == 2, 6.0, jnp.where(length == 3, 4.0, 3.0)))
            value = jnp.broadcast_to(value, (bs, 128))
            place = pl.ds(pl.multiple_of((source * XLO + x_of) * 128, 128), 128)
            ids = [jnp.broadcast_to(one, (bs, 128)) - rows for one in ids]
            for rb in range(columns):
                weight = jnp.zeros((bs, 128), F32)
                for one in ids:
                    weight = weight + jnp.where(one == rb * bs, value, 0.0)
                onehot[i, rb, :, place] = weight.astype(BF16)

    loop(0, shares * columns, weigh)

    def product(h, p):
        i, rb = p // columns, p % columns
        columns_of = raw[h, :, i].reshape(onehot.shape[3], 128)
        return jnp.dot(onehot[i, rb], columns_of, preferred_element_type=F32)

    def send_up(h, t):
        remote(
            up.at[h, t], up.at[h, t + 1], send_sem.at[4], up_sem.at[h, t + 1], along_z((z + 1) % depth)
        ).start()

    def send_down(h, t):
        remote(
            down.at[h, t], down.at[h, t + 1], send_sem.at[5], down_sem.at[h, t + 1], along_z((z + depth - 1) % depth)
        ).start()

    def piece_up(t):
        return (z + half - t + depth) % depth

    def piece_down(t):
        return (z - (half - 1) + t + depth) % depth

    def wait_up(h, t):
        drain(up.at[h, t], up_sem.at[h, t])

    def wait_down(h, t):
        drain(down.at[h, t], down_sem.at[h, t])

    for h in range(HALVES):
        drain(raw.at[h], raw_sem.at[h])
        up[h, 0] = product(h, piece_up(0))
        send_up(h, 0)
        down[h, 0] = product(h, piece_down(0))
        send_down(h, 0)

    def hop(t):
        for h in range(HALVES):
            first, second = product(h, piece_up(t)), product(h, piece_down(t))
            wait_up(h, t)
            up[h, t] += first
            send_up(h, t)
            wait_down(h, t)
            down[h, t] += second
            send_down(h, t)

    def dense_one():
        drain(xr, dense_sem.at[0])
        drain(yr, dense_sem.at[1])
        x_all = xr[...].reshape(onehot.shape[3], bs)
        y_all = yr[...].reshape(onehot.shape[3], bs)
        partial = lax.dot_general(x_all, y_all, (((0,), (0,)), ((), ())), preferred_element_type=F32)
        part[...] = partial.reshape(part.shape)

        def one(o):
            z_of = (z + o) % depth
            remote(part.at[z_of], parts.at[z], send_sem.at[6], parts_sem, along_z(z_of)).start()

        loop(1, depth, one)

    def dense_two():
        drain(parts.at[0 : depth - 1], parts_sem)
        parts[z] = part[z]
        own_sum[...] = jnp.sum(parts[...], axis=0)

        def one(o):
            remote(own_sum, grad.at[z], send_sem.at[7], grad_sem, along_z((z + o) % depth)).start()

        loop(1, depth, one)

    def dense_three():
        drain(grad.at[0 : depth - 1], grad_sem)
        grad[z] = own_sum[...]
        block = grad[...].reshape(bs, bs)
        moment_here = moment_ref[0, :, pl.ds(pl.multiple_of(g * bs, bs), bs)]
        moment = second_beta * moment_here + (1.0 - second_beta) * block * block
        graft = block / (jnp.sqrt(moment) + graft_epsilon)
        halfway = jnp.dot(left_root_ref[g, 0], block, precision=highest, preferred_element_type=F32)
        precond = jnp.dot(halfway, right_root_ref[g, 0], precision=highest, preferred_element_type=F32)
        ratio = jnp.sqrt(jnp.sum(graft * graft) / (jnp.sum(precond * precond) + norm_epsilon))
        block_update[...] = (precond * ratio).astype(BF16)
        place = update_ref.at[:, pl.ds(pl.multiple_of(me * bs, bs), bs)]
        pltpu.make_async_copy(block_update, place, update_sem).start()

        def one(o):
            remote(block_update, place, send_sem.at[8], update_sem, in_plane((me + o) % plane)).start()

        loop(1, plane, one)
        mmat[...] = moment
        lmat[...] = lax.dot_general(
            block, block, (((1,), (1,)), ((), ())), precision=highest, preferred_element_type=F32
        )
        rmat[...] = lax.dot_general(
            block, block, (((0,), (0,)), ((), ())), precision=highest, preferred_element_type=F32
        )
        stage[...] = jnp.zeros(stage.shape, F32)

        def rows_for(o):
            other = (g + o) % GROUP
            first = dp_of(other // CORES, z, other % CORES) * share
            for kind, matrix in enumerate((lmat, rmat, mmat)):
                for r in range(share):
                    stage[other, kind, r : r + 1, :] = matrix[pl.ds(first + r, 1), :]

        loop(0, GROUP, rows_for)

        def one_group(o):
            other = (g + o) % GROUP
            remote(stage.at[other], stats.at[g], send_sem.at[9], stats_sem, in_plane(blk * GROUP + other)).start()

        loop(1, GROUP, one_group)

    def dense_four():
        drain(stats.at[0 : GROUP - 1], stats_sem)
        stats[g] = stage[g]
        for other in range(GROUP):
            left_ref[other, 0] = left_stats_ref[other, 0] + stats[other, 0, 0:share, :]
            right_ref[other, 0] = right_stats_ref[other, 0] + stats[other, 1, 0:share, :]
            moment_new_ref[0, :, other * bs : (other + 1) * bs] = stats[other, 2, 0:share, :]

    steps = half - 1
    cut_one = min(2, steps)
    cut_two = min(5, steps)
    dense_one()
    loop(1, cut_one, hop)
    dense_two()
    loop(cut_one, cut_two, hop)
    dense_three()
    loop(cut_two, steps, hop)

    for h in range(HALVES):
        first, second = product(h, piece_up(half - 1)), product(h, z)
        wait_up(h, half - 1)
        up[h, half - 1] += first
        send_up(h, half - 1)
        wait_down(h, half - 1)
        final[h] = down[h, half - 1] + second
    for h in range(HALVES):
        wait_up(h, half)
        final[h] = (final[h] + up[h, half]) * (1.0 / 12.0)
        place = table_ref.at[:, h * 128 : (h + 1) * 128]

        @pl.when(piece_self)
        def _():
            pltpu.make_async_copy(final.at[h], place, table_sem).start()

        @pl.when(jnp.logical_not(piece_self))
        def _():
            remote(final.at[h], place, send_sem.at[10], table_sem, (dp_of(xl, piece_z, core), piece_blk)).start()

    dense_four()
    drain(update_ref, update_sem)
    drain(table_ref, table_sem)

    @pl.when(ids_self)
    def _():
        drain(ids_ref.at[0 : depth - 1], send_sem.at[0])

    @pl.when(jnp.logical_not(ids_self))
    def _():
        drain(ids_ref, send_sem.at[0])

    for h in range(HALVES):
        drain(raw.at[h, 0 : plane - 1], send_sem.at[1])
    drain(xr.at[0 : plane - 1], send_sem.at[2])
    drain(yr.at[0 : plane - 1], send_sem.at[3])
    drain(up.at[:, 0:half], send_sem.at[4])
    if half > 1:
        drain(down.at[:, 0 : half - 1], send_sem.at[5])
    drain(parts.at[0 : depth - 1], send_sem.at[6])
    drain(grad.at[0 : depth - 1], send_sem.at[7])
    drain(update_ref.at[:, 0 : (plane - 1) * bs], send_sem.at[8])
    drain(stats.at[0 : GROUP - 1], send_sem.at[9])

    @pl.when(jnp.logical_not(piece_self))
    def _():
        drain(final, send_sem.at[10])


def per_device(
    pooled_grad,
    bag_ids,
    bag_lengths,
    slot_table,
    layer_input,
    layer_grad_out,
    left_stats,
    right_stats,
    left_root,
    right_root,
    second_moment,
):
    depth = lax.axis_size("dp") // GROUP
    columns = lax.axis_size("blk")
    plane = columns * GROUP
    shares = depth // columns
    half = depth // 2
    samples, tables, edim = pooled_grad.shape
    width = edim // HALVES
    bs = left_root.shape[2]
    share = left_stats.shape[2]
    kdim = layer_input.shape[1]
    ids = jnp.transpose(bag_ids, (0, 1, 2, 4, 3)).reshape(tables, POOL, samples)
    lengths = bag_lengths.reshape(tables, samples)
    vmem = pl.BlockSpec(memory_space=pltpu.VMEM)
    smem = pl.BlockSpec(memory_space=pltpu.SMEM)
    hbm = pl.BlockSpec(memory_space=pl.ANY)
    raw, masked = pl.pallas_call(
        functools.partial(arrange_kernel, depth, columns),
        out_shape=(
            jax.ShapeDtypeStruct((HALVES, plane, shares, samples, width), BF16),
            jax.ShapeDtypeStruct((depth, XLO * POOL, CORES * samples), jnp.int32),
        ),
        in_specs=[smem, vmem, vmem, vmem],
        out_specs=(vmem, vmem),
        scratch_shapes=[pltpu.VMEM((HALVES, samples * tables, width), F32)],
        compiler_params=pltpu.CompilerParams(vmem_limit_bytes=32 * 1024 * 1024),
        name="arrange",
    )(slot_table, pooled_grad, ids, lengths)
    dma = pltpu.SemaphoreType.DMA
    table, left_new, right_new, moment_new, update = pl.pallas_call(
        functools.partial(main_kernel, depth, columns),
        out_shape=(
            jax.ShapeDtypeStruct((bs, edim), F32),
            jax.ShapeDtypeStruct(left_stats.shape, F32),
            jax.ShapeDtypeStruct(right_stats.shape, F32),
            jax.ShapeDtypeStruct((1, share, GROUP * bs), F32),
            jax.ShapeDtypeStruct((bs, plane * bs), BF16),
        ),
        in_specs=[hbm, hbm, hbm, hbm, vmem, vmem, vmem, vmem, vmem],
        out_specs=(hbm, vmem, vmem, vmem, hbm),
        scratch_shapes=[
            pltpu.VMEM((shares, columns, XLO * POOL, CORES * samples), jnp.int32),
            pltpu.VMEM((shares, columns, bs, plane * samples), BF16),
            pltpu.VMEM((HALVES, plane, shares, samples, width), BF16),
            pltpu.VMEM((HALVES, half + 1, bs, width), F32),
            pltpu.VMEM((HALVES, half, bs, width), F32),
            pltpu.VMEM((HALVES, bs, width), F32),
            pltpu.VMEM((plane, samples, kdim), BF16),
            pltpu.VMEM((plane, samples, bs), BF16),
            pltpu.VMEM((depth, bs // depth, bs), F32),
            pltpu.VMEM((depth, bs // depth, bs), F32),
            pltpu.VMEM((bs // depth, bs), F32),
            pltpu.VMEM((depth, bs // depth, bs), F32),
            pltpu.VMEM((bs, bs), F32),
            pltpu.VMEM((bs, bs), F32),
            pltpu.VMEM((bs, bs), F32),
            pltpu.VMEM((GROUP, 3, 8, bs), F32),
            pltpu.VMEM((GROUP, 3, 8, bs), F32),
            pltpu.VMEM((bs, bs), BF16),
            dma,
            dma((HALVES,)),
            dma((2,)),
            dma((HALVES, half + 1)),
            dma((HALVES, half)),
            dma,
            dma,
            dma,
            dma,
            dma,
            dma((11,)),
        ],
        compiler_params=pltpu.CompilerParams(
            collective_id=0, has_side_effects=True, vmem_limit_bytes=48 * 1024 * 1024
        ),
        name="exchange",
    )(
        raw,
        masked,
        layer_input,
        layer_grad_out,
        left_stats,
        right_stats,
        left_root,
        right_root,
        second_moment,
    )
    return table[None], left_new, right_new, moment_new, update[None]


def solution(mesh):
    placed = (
        P(("dp", "blk"), None, None),
        P("dp", None, "blk", None, None),
        P("dp", None, "blk", None),
        P(),
        P(("dp", "blk"), None),
        P(("dp", "blk"), None),
        P("blk", None, "dp", None),
        P("blk", None, "dp", None),
        P("blk", None, None, None),
        P("blk", None, None, None),
        P(None, None, "blk"),
    )
    return jax.shard_map(
        per_device,
        mesh=mesh,
        in_specs=placed,
        out_specs=(
            P("dp", "blk", None),
            P("blk", None, "dp", None),
            P("blk", None, "dp", None),
            P(None, "dp", "blk"),
            P(),
        ),
        check_vma=False,
    )
```

time: 911 us -> 132 us (0.14)
  the two profiles are of different devices: /device:TPU:24 before, /device:TPU:8 now
where the time goes in v1:
time: 132 us
  Pallas kernels  124 us (94%)
  local copies, waits for them, and re-layouts  7.33 us (6%)
    pallas_call x1, Pallas kernels, per_device(): pl.pallas_call(functools.partial(main_kernel, depth, columns), out_shape=...  116 us
    unnamed x27, local copies, waits for them, and re-layouts  7.33 us
    pallas_call x1, Pallas kernels, per_device(): pl.pallas_call(functools.partial(arrange_kernel, depth, columns), out_sha...  7.16 us

profile of v1, /device:TPU:8, one launch (start us, length us, event | category | flops | bytes accessed | tf_op | source)
XLA Modules:
  0.0 131.6 jit_solution(8107280701880450186)
XLA Ops:
  0.6 0.0 copy-start
  0.6 1.6 %copy-done = bf16[64,64,256]{2,1,0:T(8,128)(2,1)S(1)} copy-done((bf16[64,64,256]{2,1,0:T(8,128)(2,1)S(1)}, bf16[64,64,256]{2,1,0:T(8,128)(2,1)}, u32[]{:S(2)}) %copy-start) | copy-done | bytes 2097176
  2.2 0.0 copy-start.5
  2.2 0.9 copy-done.5
  3.1 0.0 copy-start.6
  3.1 0.8 copy-done.6
  3.9 0.0 copy-start.10
  3.9 0.7 copy-done.10
  4.5 0.0 copy-start.1
  4.5 0.0 copy-start.2
  4.6 0.0 copy-start.3
  4.6 0.0 copy-start.4
  4.6 0.0 copy-start.7
  4.6 0.0 copy-start.8
  4.6 0.0 copy-start.9
  4.6 7.2 %arrange.1 = (bf16[2,32,2,64,128]{4,3,2,1,0:T(8,128)(2,1)S(1)}, s32[16,8,128]{2,1,0:T(8,128)S(1)}) custom-call(s32[64]{0:T(128)S(1)} %copy-done.10, bf16[64,64,256]{2,1,0:T(8,128)(2,1)S(1)} %copy-done, s32[64,4,64]{2,1,0:T(4,128)S(1)} %bitcast.9, s32[64,64]{1,0:T(8,128)S(1)} %bitcast.11), custom_call_target="tpu_custom_call" | custom-call | tf_op jit(solution)/shard_map/arrange/pallas_call | solution.py:444
  11.7 0.0 copy-done.1
  11.7 0.0 copy-done.2
  11.7 0.0 copy-done.3
  11.8 0.0 copy-done.4
  11.8 0.0 copy-done.7
  11.8 0.0 copy-done.8
  11.8 0.0 copy-done.9
  11.8 116.4 %exchange.1 = (f32[128,256]{1,0:T(8,128)S(1)}, f32[4,1,2,128]{3,2,1,0:T(2,128)S(1)}, f32[4,1,2,128]{3,2,1,0:T(2,128)S(1)}, f32[1,2,512]{2,1,0:T(2,128)S(1)}, bf16[128,4096]{1,0:T(8,128)(2,1)S(1)}) custom-call(bf16[2,32,2,64,128]{4,3,2,1,0:T(8,128)(2,1)S(1)} %get-tuple-element.12.raw_ref, s32[16,8,128]{2,1,0:T(8,128)S(1)} %get-tuple-element.13.ids_ref, ...), custom_call_target="tpu_custom_call" | custom-call | tf_op jit(solution)/shard_map/exchange/pallas_call | solution.py:457
  128.2 0.7 copy.22
  128.9 0.6 copy.23
  129.4 0.6 copy.24
  130.0 0.6 copy.25
  130.6 1.0 copy.26
Async XLA Ops:
  0.6 1.6 %copy-start = (bf16[64,64,256]{2,1,0:T(8,128)(2,1)S(1)}, bf16[64,64,256]{2,1,0:T(8,128)(2,1)}, u32[]{:S(2)}) copy-start(bf16[64,64,256]{2,1,0:T(8,128)(2,1)} %x_ref.2) | copy-start | bytes 6291460
  2.2 0.9 copy-start.5
  3.1 0.8 copy-start.6
  3.9 0.7 copy-start.10
  4.5 7.2 %copy-start.1 = (bf16[64,4096]{1,0:T(8,128)(2,1)S(1)}, bf16[64,4096]{1,0:T(8,128)(2,1)}, u32[]{:S(2)}) copy-start(bf16[64,4096]{1,0:T(8,128)(2,1)} %y_ref.1) | copy-start | bytes 1572868
  4.5 7.2 %copy-start.2 = (f32[4,1,128,128]{3,2,1,0:T(8,128)S(1)}, f32[4,1,128,128]{3,2,1,0:T(8,128)}, u32[]{:S(2)}) copy-start(f32[4,1,128,128]{3,2,1,0:T(8,128)} %left_root_ref.1) | copy-start | bytes 786436
  4.6 7.2 %copy-start.3 = (f32[4,1,128,128]{3,2,1,0:T(8,128)S(1)}, f32[4,1,128,128]{3,2,1,0:T(8,128)}, u32[]{:S(2)}) copy-start(f32[4,1,128,128]{3,2,1,0:T(8,128)} %right_root_ref.1) | copy-start | bytes 786436
  4.6 7.2 %copy-start.4 = (f32[1,128,512]{2,1,0:T(8,128)S(1)}, f32[1,128,512]{2,1,0:T(8,128)}, u32[]{:S(2)}) copy-start(f32[1,128,512]{2,1,0:T(8,128)} %moment_ref.1) | copy-start | bytes 786436
  4.6 7.2 %copy-start.7 = (bf16[64,128]{1,0:T(8,128)(2,1)S(1)}, bf16[64,128]{1,0:T(8,128)(2,1)}, u32[]{:S(2)}) copy-start(bf16[64,128]{1,0:T(8,128)(2,1)} %x_ref.3) | copy-start | bytes 49156
  4.6 7.2 %copy-start.8 = (f32[4,1,2,128]{3,2,1,0:T(2,128)S(1)}, f32[4,1,2,128]{3,2,1,0:T(2,128)}, u32[]{:S(2)}) copy-start(f32[4,1,2,128]{3,2,1,0:T(2,128)} %left_stats_ref.1) | copy-start | bytes 12292
  4.6 7.2 %copy-start.9 = (f32[4,1,2,128]{3,2,1,0:T(2,128)S(1)}, f32[4,1,2,128]{3,2,1,0:T(2,128)}, u32[]{:S(2)}) copy-start(f32[4,1,2,128]{3,2,1,0:T(2,128)} %right_stats_ref.1) | copy-start | bytes 12292

commit v2 on v1

v2 whole, which is shorter than its diff:
```python
import functools

import jax
import jax.numpy as jnp
from jax import lax
from jax.experimental import pallas as pl
from jax.experimental.pallas import tpu as pltpu
from jax.sharding import PartitionSpec as P

MESH = pl.DeviceIdType.MESH
F32, BF16 = jnp.float32, jnp.bfloat16
CORES, XLO = 2, 2
GROUP = CORES * XLO
POOL = 4
HALVES = 2
LAG = 5
DENSE_AT = (2, 3, 5, 7, 8, 10, 13)
SUBS = 4

second_beta = 0.9
graft_epsilon = 1e-08
norm_epsilon = 1e-06
highest = lax.Precision.HIGHEST


def exchange_kernel(
    depth,
    columns,
    slots_ref,
    pooled_ref,
    ids_ref,
    lengths_ref,
    x_ref,
    y_ref,
    left_stats_ref,
    right_stats_ref,
    left_root_ref,
    right_root_ref,
    moment_ref,
    table_ref,
    left_ref,
    right_ref,
    moment_new_ref,
    update_ref,
    pooled,
    wide,
    ordered,
    ids_in,
    lengths_in,
    masked,
    idr,
    onehot,
    raw,
    own,
    up,
    down,
    final,
    xr,
    yr,
    part,
    parts,
    own_sum,
    grad,
    lmat,
    rmat,
    mmat,
    stage,
    stats,
    block_update,
    left_root,
    right_root,
    moment_in,
    left_stats,
    right_stats,
    left_out,
    right_out,
    moment_out,
    pooled_sem,
    in_sem,
    out_sem,
    ids_sem,
    raw_sem,
    x_sem,
    y_sem,
    up_sem,
    down_sem,
    table_sem,
    parts_sem,
    grad_sem,
    stats_sem,
    update_sem,
    passed_sem,
    send_sem,
):
    plane = columns * GROUP
    chips = plane // CORES
    shares = depth // columns
    half = depth // 2
    bs = lmat.shape[0]
    share = left_ref.shape[2]
    samples, tables, edim = pooled.shape
    width = edim // HALVES
    kdim = plane * samples
    dp, blk = lax.axis_index("dp"), lax.axis_index("blk")
    core = dp % CORES
    z = (dp // CORES) % depth
    xl = dp // (CORES * depth)
    g = xl * CORES + core
    me = blk * GROUP + g
    chip = me // CORES

    def dp_of(xl_of, z_of, core_of):
        return (xl_of * depth + z_of) * CORES + core_of

    def in_plane(q):
        other = q % GROUP
        return (dp_of(other // CORES, z, other % CORES), q // GROUP)

    def along_z(z_of):
        return (dp_of(xl, z_of, core), blk)

    def same_core(chip_of):
        return in_plane(chip_of * CORES + core)

    twin = in_plane(chip * CORES + 1 - core)

    def loop(first, last, body):
        def step(k, carry):
            body(k)
            return carry

        lax.fori_loop(first, last, step, 0)

    def remote(src, dst, sent, arrived, device):
        return pltpu.make_async_remote_copy(
            src_ref=src, dst_ref=dst, send_sem=sent, recv_sem=arrived, device_id=device, device_id_type=MESH
        )

    def drain(ref, sem):
        pltpu.make_async_copy(ref, ref, sem).wait()

    chunks = pooled_sem.shape[0]
    per_chunk = samples // chunks

    def pooled_copy(k):
        rows = pl.ds(k * per_chunk, per_chunk)
        return pltpu.make_async_copy(pooled_ref.at[rows], pooled.at[rows], pooled_sem.at[k])

    local = [
        pltpu.make_async_copy(src, dst, in_sem.at[k])
        for k, (src, dst) in enumerate(
            (
                (ids_ref, ids_in),
                (lengths_ref, lengths_in),
                (left_root_ref.at[g, 0], left_root),
                (right_root_ref.at[g, 0], right_root),
                (moment_ref.at[0, :, pl.ds(pl.multiple_of(g * bs, bs), bs)], moment_in),
                (left_stats_ref, left_stats),
                (right_stats_ref, right_stats),
            )
        )
    ]
    loop(0, chunks, lambda k: pooled_copy(k).start())
    for copy in local:
        copy.start()

    ids_self = blk == z // shares
    piece_z = blk * shares + z // columns
    piece_blk = z % columns
    piece_self = jnp.logical_and(piece_z == z, piece_blk == blk)
    from_z = (z % shares) * columns + blk
    from_blk = z // shares

    barrier = pltpu.get_barrier_semaphore()

    def greet(device):
        pl.semaphore_signal(barrier, inc=1, device_id=device, device_id_type=MESH)

    loop(1, plane, lambda o: greet(in_plane((me + o) % plane)))
    loop(1, depth, lambda o: greet(along_z((z + o) % depth)))

    def greet_ids(k):
        z_of, blk_of = blk * shares + k // columns, k % columns

        @pl.when(jnp.logical_not(jnp.logical_and(z_of == z, blk_of == blk)))
        def _():
            greet((dp_of(xl, z_of, core), blk_of))

    loop(0, depth, greet_ids)

    @pl.when(jnp.logical_not(piece_self))
    def _():
        greet((dp_of(xl, from_z, core), from_blk))

    local[0].wait()
    local[1].wait()
    position = lax.broadcasted_iota(jnp.int32, (POOL, samples), 0)

    def mask(z_of):
        for x_of in range(XLO):
            for core_of in range(CORES):
                source = dp_of(x_of, z_of, core_of)
                bag = lengths_in[pl.ds(source, 1), :]
                kept = jnp.where(position < bag, ids_in[source], -1)
                masked[z_of, x_of * POOL : (x_of + 1) * POOL, core_of * samples : (core_of + 1) * samples] = kept

    loop(0, depth, mask)

    def widen(h):
        def one(s):
            rows = pl.ds(pl.multiple_of(s * tables, tables), tables)
            wide[h, rows, :] = pooled[s, :, h * width : (h + 1) * width].astype(F32)

        return one

    def widen_first(k):
        pooled_copy(k).wait()
        loop(k * per_chunk, (k + 1) * per_chunk, widen(0))

    loop(0, chunks, widen_first)

    greetings = (plane - 1) + (depth - 1) + depth + 1
    pl.semaphore_wait(barrier, greetings - ids_self.astype(jnp.int32) - piece_self.astype(jnp.int32))

    def send_ids(k):
        z_of = (z + k) % depth
        itself = jnp.logical_and(z_of == z, ids_self)
        place = idr.at[z % shares, blk]

        @pl.when(itself)
        def _():
            pltpu.make_async_copy(masked.at[z_of], place, ids_sem).start()

        @pl.when(jnp.logical_not(itself))
        def _():
            remote(masked.at[z_of], place, send_sem.at[0], ids_sem, (dp_of(xl, z_of, core), z // shares)).start()

    loop(0, depth, send_ids)

    def rows_of(h, q, i):
        other = q % GROUP
        slot = dp_of(other // CORES, (q // GROUP) * shares + i, other % CORES)
        return wide[h, pl.ds(slots_ref[slot], samples, stride=tables), :].astype(BF16)

    def send_raw(h):
        def one(o):
            q = (me + o) % plane
            for i in range(shares):
                ordered[h, q, i] = rows_of(h, q, i)
            remote(ordered.at[h, q], raw.at[h, me], send_sem.at[1], raw_sem.at[h], in_plane(q)).start()

        loop(1, plane, one)
        for i in range(shares):
            raw[h, me, i] = rows_of(h, me, i)

    def send_dense():
        def y_part(q):
            return y_ref.at[:, pl.ds(pl.multiple_of(q * bs, bs), bs)]

        pltpu.make_async_copy(x_ref, xr.at[core, chip], x_sem.at[0]).start()
        pltpu.make_async_copy(y_part(me), yr.at[core, chip], y_sem).start()

        def one_x(o):
            remote(x_ref, xr.at[core, chip], send_sem.at[2], x_sem.at[0], same_core((chip + o) % chips)).start()

        def one_y(o):
            q = (me + o) % plane
            remote(y_part(q), yr.at[core, chip], send_sem.at[3], y_sem, in_plane(q)).start()

        loop(1, chips, one_x)
        loop(1, plane, one_y)

    send_raw(0)
    send_dense()
    loop(0, samples, widen(1))
    send_raw(1)

    drain(idr, ids_sem)
    rows = lax.broadcasted_iota(jnp.int32, (bs, 128), 0)

    def weigh(k):
        i, source = k // columns, k % columns
        tile = idr[i, source]
        for x_of in range(XLO):
            ids = [tile[x_of * POOL + p : x_of * POOL + p + 1, :] for p in range(POOL)]
            length = sum((one >= 0).astype(jnp.int32) for one in ids)
            value = jnp.where(length == 1, 12.0, jnp.where(length == 2, 6.0, jnp.where(length == 3, 4.0, 3.0)))
            value = jnp.broadcast_to(value, (bs, 128))
            place = pl.ds(pl.multiple_of((source * XLO + x_of) * 128, 128), 128)
            ids = [jnp.broadcast_to(one, (bs, 128)) - rows for one in ids]
            for rb in range(columns):
                weight = jnp.zeros((bs, 128), F32)
                for one in ids:
                    weight = weight + jnp.where(one == rb * bs, value, 0.0)
                onehot[i, rb * bs : (rb + 1) * bs, place] = weight.astype(BF16)

    loop(0, shares * columns, weigh)

    def product(h, i):
        whole = jnp.dot(onehot[i], raw[h, :, i].reshape(kdim, width), preferred_element_type=F32)
        own[h, pl.ds(i * columns, columns)] = whole.reshape(columns, bs, width)

    def product_of(h, p):
        i, rb = p // columns, p % columns
        weights = onehot[i, pl.ds(pl.multiple_of(rb * bs, bs), bs), :]
        own[h, p] = jnp.dot(weights, raw[h, :, i].reshape(kdim, width), preferred_element_type=F32)

    sub = bs // SUBS

    def rows_at(s):
        return pl.ds(s * sub, sub)

    def send_up(h, t, s):
        there = up.at[h, t + 1, rows_at(s)]
        remote(
            up.at[h, t, rows_at(s)], there, send_sem.at[4], up_sem.at[h, t + 1, s], along_z((z + 1) % depth)
        ).start()

    def send_down(h, t, s):
        there = down.at[h, t + 1, rows_at(s)]
        remote(
            down.at[h, t, rows_at(s)], there, send_sem.at[5], down_sem.at[h, t + 1, s], along_z((z + depth - 1) % depth)
        ).start()

    def piece_up(t):
        return (z + half - t + depth) % depth

    def piece_down(t):
        return (z - (half - 1) + t + depth) % depth

    def wait_up(h, t, s):
        drain(up.at[h, t, rows_at(s)], up_sem.at[h, t, s])

    def wait_down(h, t, s):
        drain(down.at[h, t, rows_at(s)], down_sem.at[h, t, s])

    def begin(h):
        drain(raw.at[h, 0 : plane - 1], raw_sem.at[h])
        for k in range(shares):
            if h == 0:
                product(h, (piece_up(0) // columns + k) % shares)
            elif k == 0:
                product_of(h, piece_up(0))
            if k == 0:
                up[h, 0] = own[h, piece_up(0)]
                for s in range(SUBS):
                    send_up(h, 0, s)
        if h > 0:
            product_of(h, piece_down(0))
        down[h, 0] = own[h, piece_down(0)]
        if half > 1:
            for s in range(SUBS):
                send_down(h, 0, s)

    def hop(h, t):
        if h > 0:
            product_of(h, piece_up(t))
            product_of(h, piece_down(t))
        for s in range(SUBS):
            wait_up(h, t, s)
            up[h, t, rows_at(s)] += own[h, piece_up(t), rows_at(s)]
            send_up(h, t, s)
            wait_down(h, t, s)
            down[h, t, rows_at(s)] += own[h, piece_down(t), rows_at(s)]
            send_down(h, t, s)

    def last(h):
        t = half - 1
        if h > 0:
            product_of(h, piece_up(t))
            product_of(h, z)
        for s in range(SUBS):
            wait_up(h, t, s)
            up[h, t, rows_at(s)] += own[h, piece_up(t), rows_at(s)]
            send_up(h, t, s)
        for s in range(SUBS):
            wait_down(h, t, s)
            final[h, rows_at(s)] = down[h, t, rows_at(s)] + own[h, z, rows_at(s)]

    def finish(h):
        for s in range(SUBS):
            wait_up(h, half, s)
            final[h, rows_at(s)] = (final[h, rows_at(s)] + up[h, half, rows_at(s)]) * (1.0 / 12.0)
            piece = final.at[h, rows_at(s)]
            place = table_ref.at[rows_at(s), h * width : (h + 1) * width]

            @pl.when(piece_self)
            def _(piece=piece, place=place):
                pltpu.make_async_copy(piece, place, table_sem).start()

            @pl.when(jnp.logical_not(piece_self))
            def _(piece=piece, place=place):
                remote(piece, place, send_sem.at[10], table_sem, (dp_of(xl, piece_z, core), piece_blk)).start()

    def pass_input():
        drain(xr.at[core], x_sem.at[0])
        remote(xr.at[core], xr.at[core], send_sem.at[11], x_sem.at[1], twin).start()

    def dense_one():
        drain(yr, y_sem)
        drain(xr.at[core], x_sem.at[1])
        partial = lax.dot_general(
            xr[...].reshape(kdim, bs),
            yr[...].reshape(kdim, bs),
            (((0,), (0,)), ((), ())),
            preferred_element_type=F32,
        )
        part[...] = partial.reshape(part.shape)

        def one(o):
            z_of = (z + o) % depth
            remote(part.at[z_of], parts.at[z], send_sem.at[6], parts_sem, along_z(z_of)).start()

        loop(1, depth, one)

    def dense_two():
        drain(parts.at[0 : depth - 1], parts_sem)
        parts[z] = part[z]
        own_sum[...] = jnp.sum(parts[...], axis=0)

        def one(o):
            remote(own_sum, grad.at[z], send_sem.at[7], grad_sem, along_z((z + o) % depth)).start()

        loop(1, depth, one)

    def block_place(q):
        return update_ref.at[:, pl.ds(pl.multiple_of(q * bs, bs), bs)]

    def dense_three():
        drain(grad.at[0 : depth - 1], grad_sem)
        grad[z] = own_sum[...]
        block = grad[...].reshape(bs, bs)
        for copy in local[2:5]:
            copy.wait()
        moment = second_beta * moment_in[...] + (1.0 - second_beta) * block * block
        graft = block / (jnp.sqrt(moment) + graft_epsilon)
        halfway = jnp.dot(left_root[...], block, precision=highest, preferred_element_type=F32)
        precond = jnp.dot(halfway, right_root[...], precision=highest, preferred_element_type=F32)
        ratio = jnp.sqrt(jnp.sum(graft * graft) / (jnp.sum(precond * precond) + norm_epsilon))
        block_update[...] = (precond * ratio).astype(BF16)
        place = block_place(me)

        def one(o):
            remote(block_update, place, send_sem.at[8], update_sem.at[o], same_core((chip + o) % chips)).start()

        loop(1, chips, one)
        remote(block_update, place, send_sem.at[8], passed_sem, twin).start()
        pltpu.make_async_copy(block_update, place, update_sem.at[0]).start()
        mmat[...] = moment

    def statistics():
        block = grad[...].reshape(bs, bs)
        lmat[...] = lax.dot_general(
            block, block, (((1,), (1,)), ((), ())), precision=highest, preferred_element_type=F32
        )
        rmat[...] = lax.dot_general(
            block, block, (((0,), (0,)), ((), ())), precision=highest, preferred_element_type=F32
        )
        stage[...] = jnp.zeros(stage.shape, F32)

        def rows_for(o):
            other = (g + o) % GROUP
            first = dp_of(other // CORES, z, other % CORES) * share
            for kind, matrix in enumerate((lmat, rmat, mmat)):
                for r in range(share):
                    stage[other, kind, r : r + 1, :] = matrix[pl.ds(first + r, 1), :]

        loop(0, GROUP, rows_for)

        def one_group(o):
            other = (g + o) % GROUP
            remote(stage.at[other], stats.at[g], send_sem.at[9], stats_sem, in_plane(blk * GROUP + other)).start()

        loop(1, GROUP, one_group)

    def pass_update():
        def one(o):
            place = block_place(((chip + chips - o) % chips) * CORES + core)
            pltpu.make_async_copy(place, place, update_sem.at[o]).wait()
            remote(place, place, send_sem.at[8], passed_sem, twin).start()

        loop(1, chips, one)

    results = (
        pltpu.make_async_copy(left_out, left_ref, out_sem.at[0]),
        pltpu.make_async_copy(right_out, right_ref, out_sem.at[1]),
        pltpu.make_async_copy(moment_out, moment_new_ref, out_sem.at[2]),
    )

    def store_statistics():
        local[5].wait()
        local[6].wait()
        drain(stats.at[0 : GROUP - 1], stats_sem)
        stats[g] = stage[g]
        for other in range(GROUP):
            left_out[other, 0] = left_stats[other, 0] + stats[other, 0, 0:share, :]
            right_out[other, 0] = right_stats[other, 0] + stats[other, 1, 0:share, :]
            moment_out[0, :, other * bs : (other + 1) * bs] = stats[other, 2, 0:share, :]
        for copy in results:
            copy.start()

    lag = min(LAG, half + 1)
    end = half + lag
    dense = {}
    parts_of_dense = (pass_input, dense_one, dense_two, dense_three, statistics, pass_update, store_statistics)
    for at, part_of in zip(DENSE_AT, parts_of_dense):
        dense.setdefault(min(at, end), []).append(part_of)

    def kind(t):
        return "" if t < 0 or t > half else "b" if t == 0 else "f" if t == half else "l" if t == half - 1 else "h"

    step = 0
    while step <= end:
        kinds = (kind(step), kind(step - lag))
        stop = step + 1
        while stop <= end and "h" in kinds and (kind(stop), kind(stop - lag)) == kinds and not dense.get(stop - 1):
            stop += 1

        def run(t, kinds=kinds):
            for h, what in enumerate(kinds):
                if what == "b":
                    begin(h)
                elif what == "h":
                    hop(h, t - h * lag)
                elif what == "l":
                    last(h)
                elif what == "f":
                    finish(h)

        if stop - step > 1:
            loop(step, stop, run)
        else:
            run(step)
        for part_of in dense.get(stop - 1, ()):
            part_of()
        step = stop

    drain(table_ref, table_sem)
    drain(block_place(me), update_sem.at[0])
    drain(update_ref.at[:, 0 : chips * bs], passed_sem)
    for copy in results:
        copy.wait()

    @pl.when(ids_self)
    def _():
        drain(masked.at[0 : depth - 1], send_sem.at[0])

    @pl.when(jnp.logical_not(ids_self))
    def _():
        drain(masked, send_sem.at[0])

    for h in range(HALVES):
        drain(raw.at[h, 0 : plane - 1], send_sem.at[1])
    drain(xr.at[0, 0 : chips - 1], send_sem.at[2])
    drain(xr.at[0], send_sem.at[11])
    drain(yr.at[0, 0 : chips - 1], send_sem.at[3])
    drain(yr.at[0], send_sem.at[3])
    drain(up.at[:, 0:half], send_sem.at[4])
    if half > 1:
        drain(down.at[:, 0 : half - 1], send_sem.at[5])
    drain(parts.at[0 : depth - 1], send_sem.at[6])
    drain(grad.at[0 : depth - 1], send_sem.at[7])
    drain(update_ref.at[:, 0 : (plane - 1) * bs], send_sem.at[8])
    drain(stats.at[0 : GROUP - 1], send_sem.at[9])

    @pl.when(jnp.logical_not(piece_self))
    def _():
        drain(final, send_sem.at[10])


def place_kernel(cuts, *refs):
    count = len(cuts)
    sources, places, held, sem = refs[:count], refs[count : 2 * count], refs[2 * count : 3 * count], refs[-1]
    moves = []
    for source, place, here, cut in zip(sources, places, held, cuts):
        rows = source.shape[0] // cut
        for k in range(cut):
            at = pl.ds(k * rows, rows)
            n = len(moves)
            moves.append(
                (
                    pltpu.make_async_copy(source.at[at], here.at[at], sem.at[0, n]),
                    pltpu.make_async_copy(here.at[at], place.at[at], sem.at[1, n]),
                )
            )
    for first, _ in moves:
        first.start()
    for first, second in moves:
        first.wait()
        second.start()
    for _, second in moves:
        second.wait()


def per_device(
    pooled_grad,
    bag_ids,
    bag_lengths,
    slot_table,
    layer_input,
    layer_grad_out,
    left_stats,
    right_stats,
    left_root,
    right_root,
    second_moment,
):
    depth = lax.axis_size("dp") // GROUP
    columns = lax.axis_size("blk")
    plane = columns * GROUP
    chips = plane // CORES
    shares = depth // columns
    half = depth // 2
    samples, tables, edim = pooled_grad.shape
    width = edim // HALVES
    bs = left_root.shape[2]
    share = left_stats.shape[2]
    kdim = layer_input.shape[1]
    ids = jnp.transpose(bag_ids, (0, 1, 2, 4, 3)).reshape(tables, POOL, samples)
    lengths = bag_lengths.reshape(tables, samples)
    smem = pl.BlockSpec(memory_space=pltpu.SMEM)
    hbm = pl.BlockSpec(memory_space=pl.ANY)
    dma = pltpu.SemaphoreType.DMA
    vmem = pltpu.VMEM
    shapes = (
        jax.ShapeDtypeStruct((bs, edim), F32),
        jax.ShapeDtypeStruct(left_stats.shape, F32),
        jax.ShapeDtypeStruct(right_stats.shape, F32),
        jax.ShapeDtypeStruct((1, share, GROUP * bs), F32),
        jax.ShapeDtypeStruct((bs, plane * bs), BF16),
    )
    cuts = (1, 1, 1, 1, 4)
    results = pl.pallas_call(
        functools.partial(exchange_kernel, depth, columns),
        out_shape=shapes,
        in_specs=[smem] + [hbm] * 10,
        out_specs=(hbm,) * 5,
        scratch_shapes=[
            vmem((samples, tables, edim), BF16),
            vmem((HALVES, samples * tables, width), F32),
            vmem((HALVES, plane, shares, samples, width), BF16),
            vmem((tables, POOL, samples), jnp.int32),
            vmem((tables, samples), jnp.int32),
            vmem((depth, XLO * POOL, CORES * samples), jnp.int32),
            vmem((shares, columns, XLO * POOL, CORES * samples), jnp.int32),
            vmem((shares, columns * bs, plane * samples), BF16),
            vmem((HALVES, plane, shares, samples, width), BF16),
            vmem((HALVES, depth, bs, width), F32),
            vmem((HALVES, half + 1, bs, width), F32),
            vmem((HALVES, half, bs, width), F32),
            vmem((HALVES, bs, width), F32),
            vmem((CORES, chips, samples, kdim), BF16),
            vmem((CORES, chips, samples, bs), BF16),
            vmem((depth, bs // depth, bs), F32),
            vmem((depth, bs // depth, bs), F32),
            vmem((bs // depth, bs), F32),
            vmem((depth, bs // depth, bs), F32),
            vmem((bs, bs), F32),
            vmem((bs, bs), F32),
            vmem((bs, bs), F32),
            vmem((GROUP, 3, 8, bs), F32),
            vmem((GROUP, 3, 8, bs), F32),
            vmem((bs, bs), BF16),
            vmem((bs, bs), F32),
            vmem((bs, bs), F32),
            vmem((bs, bs), F32),
            vmem(left_stats.shape, F32),
            vmem(right_stats.shape, F32),
            vmem(left_stats.shape, F32),
            vmem(right_stats.shape, F32),
            vmem((1, share, GROUP * bs), F32),
            dma((8,)),
            dma((7,)),
            dma((3,)),
            dma,
            dma((HALVES,)),
            dma((2,)),
            dma,
            dma((HALVES, half + 1, SUBS)),
            dma((HALVES, half, SUBS)),
            dma,
            dma,
            dma,
            dma,
            dma((chips,)),
            dma,
            dma((12,)),
        ],
        compiler_params=pltpu.CompilerParams(
            collective_id=0, has_side_effects=True, vmem_limit_bytes=56 * 1024 * 1024
        ),
        name="exchange",
    )(
        slot_table,
        pooled_grad,
        ids,
        lengths,
        layer_input,
        layer_grad_out,
        left_stats,
        right_stats,
        left_root,
        right_root,
        second_moment,
    )
    table, left_new, right_new, moment_new, update = pl.pallas_call(
        functools.partial(place_kernel, cuts),
        out_shape=shapes,
        in_specs=[hbm] * 5,
        out_specs=(hbm,) * 5,
        scratch_shapes=[vmem(one.shape, one.dtype) for one in shapes] + [dma((2, sum(cuts)))],
        compiler_params=pltpu.CompilerParams(vmem_limit_bytes=56 * 1024 * 1024),
        name="place",
    )(*results)
    return table[None], left_new, right_new, moment_new, update[None]


def solution(mesh):
    placed = (
        P(("dp", "blk"), None, None),
        P("dp", None, "blk", None, None),
        P("dp", None, "blk", None),
        P(),
        P(("dp", "blk"), None),
        P(("dp", "blk"), None),
        P("blk", None, "dp", None),
        P("blk", None, "dp", None),
        P("blk", None, None, None),
        P("blk", None, None, None),
        P(None, None, "blk"),
    )
    return jax.shard_map(
        per_device,
        mesh=mesh,
        in_specs=placed,
        out_specs=(
            P("dp", "blk", None),
            P("blk", None, "dp", None),
            P("blk", None, "dp", None),
            P(None, "dp", "blk"),
            P(),
        ),
        check_vma=False,
    )
```

time: 132 us -> 108 us (0.82)
  the two profiles are of different devices: /device:TPU:8 before, /device:TPU:24 now
where the time goes in v2:
time: 108 us; the launch traced here: 106 us
  Pallas kernels  105 us (97%)
    pallas_call x1, Pallas kernels, per_device(): pl.pallas_call(functools.partial(exchange_kernel, depth, columns), out_sh...  103 us

profile of v2, /device:TPU:24, one launch (start us, length us, event | category | flops | bytes accessed | tf_op | source)
XLA Modules:
  0.0 105.9 jit_solution(17904305480129502839)
XLA Ops:
  0.6 103.1 %exchange.1 = (f32[128,256]{1,0:T(8,128)}, f32[4,1,2,128]{3,2,1,0:T(2,128)}, f32[4,1,2,128]{3,2,1,0:T(2,128)}, f32[1,2,512]{2,1,0:T(2,128)}, bf16[128,4096]{1,0:T(8,128)(2,1)}) custom-call(s32[64]{0:T(128)} %slots_ref.1, bf16[64,64,256]{2,1,0:T(8,128)(2,1)} %pooled_ref.1, s32[64,4,64]{2,1,0:T(4,128)} %bitcast.8, s32[64,64]{1,0:T(8,128)} %bitcast.9, ...), custom_call_target="tpu_custom_call" | custom-call | tf_op jit(solution)/shard_map/exchange/pallas_call | solution.py:633
  103.7 2.1 %place.1 = (f32[128,256]{1,0:T(8,128)}, f32[4,1,2,128]{3,2,1,0:T(2,128)}, f32[4,1,2,128]{3,2,1,0:T(2,128)}, f32[1,2,512]{2,1,0:T(2,128)}, bf16[128,4096]{1,0:T(8,128)(2,1)}) custom-call(f32[128,256]{1,0:T(8,128)} %get-tuple-element.15.refs_0_, f32[4,1,2,128]{3,2,1,0:T(2,128)} %get-tuple-element.16.refs_1_, f32[4,1,2,128]{3,2,1,0:T(2,128)} %get-tuple-element.17.refs_2_, ...), custom_call_target="tpu_custom_call" | custom-call | tf_op jit(solution)/shard_map/place/pallas_call | solution.py:706

commit v3 on v2

--- a/solution.py
+++ b/solution.py
@@ -13,12 +13,14 @@
 GROUP = CORES * XLO
 POOL = 4
 HALVES = 2
-LAG = 5
-DENSE_AT = (2, 3, 5, 7, 8, 10, 13)
-SUBS = 4
+LAG = 2
+SUBS = 2
+DENSE_MID = False
 
 second_beta = 0.9
 graft_epsilon = 1e-08
+tiny = 1e-30
+steps_16 = 32000.0
 norm_epsilon = 1e-06
 highest = lax.Precision.HIGHEST
 
@@ -52,9 +54,15 @@
     onehot,
     raw,
     own,
+    given,
     up,
     down,
     final,
+    coded,
+    steps_out,
+    coded_in,
+    steps_in,
+    table_out,
     xr,
     yr,
     part,
@@ -82,8 +90,11 @@
     raw_sem,
     x_sem,
     y_sem,
+    given_sem,
     up_sem,
     down_sem,
+    coded_sem,
+    steps_sem,
     table_sem,
     parts_sem,
     grad_sem,
@@ -96,7 +107,7 @@
     chips = plane // CORES
     shares = depth // columns
     half = depth // 2
-    bs = lmat.shape[0]
+    bs = lmat.shape[1]
     share = left_ref.shape[2]
     samples, tables, edim = pooled.shape
     width = edim // HALVES
@@ -108,6 +119,7 @@
     g = xl * CORES + core
     me = blk * GROUP + g
     chip = me // CORES
+    wide_bs = CORES * bs
 
     def dp_of(xl_of, z_of, core_of):
         return (xl_of * depth + z_of) * CORES + core_of
@@ -152,9 +164,9 @@
             (
                 (ids_ref, ids_in),
                 (lengths_ref, lengths_in),
-                (left_root_ref.at[g, 0], left_root),
-                (right_root_ref.at[g, 0], right_root),
-                (moment_ref.at[0, :, pl.ds(pl.multiple_of(g * bs, bs), bs)], moment_in),
+                (left_root_ref.at[pl.ds(xl * CORES, CORES), 0], left_root),
+                (right_root_ref.at[pl.ds(xl * CORES, CORES), 0], right_root),
+                (moment_ref.at[0, :, pl.ds(pl.multiple_of(xl * wide_bs, wide_bs), wide_bs)], moment_in),
                 (left_stats_ref, left_stats),
                 (right_stats_ref, right_stats),
             )
@@ -190,7 +202,7 @@
 
     @pl.when(jnp.logical_not(piece_self))
     def _():
-        greet((dp_of(xl, from_z, core), from_blk))
+        greet((dp_of(xl, from_z, 1), from_blk))
 
     local[0].wait()
     local[1].wait()
@@ -219,8 +231,8 @@
 
     loop(0, chunks, widen_first)
 
-    greetings = (plane - 1) + (depth - 1) + depth + 1
-    pl.semaphore_wait(barrier, greetings - ids_self.astype(jnp.int32) - piece_self.astype(jnp.int32))
+    greetings = (plane - 1) + (depth - 1) + depth - ids_self.astype(jnp.int32)
+    pl.semaphore_wait(barrier, greetings + CORES * core * jnp.logical_not(piece_self).astype(jnp.int32))
 
     def send_ids(k):
         z_of = (z + k) % depth
@@ -253,27 +265,34 @@
         for i in range(shares):
             raw[h, me, i] = rows_of(h, me, i)
 
+    def y_part(chip_of):
+        return y_ref.at[:, pl.ds(pl.multiple_of(chip_of * wide_bs, wide_bs), wide_bs)]
+
     def send_dense():
-        def y_part(q):
-            return y_ref.at[:, pl.ds(pl.multiple_of(q * bs, bs), bs)]
-
-        pltpu.make_async_copy(x_ref, xr.at[core, chip], x_sem.at[0]).start()
-        pltpu.make_async_copy(y_part(me), yr.at[core, chip], y_sem).start()
-
-        def one_x(o):
-            remote(x_ref, xr.at[core, chip], send_sem.at[2], x_sem.at[0], same_core((chip + o) % chips)).start()
-
-        def one_y(o):
-            q = (me + o) % plane
-            remote(y_part(q), yr.at[core, chip], send_sem.at[3], y_sem, in_plane(q)).start()
-
-        loop(1, chips, one_x)
-        loop(1, plane, one_y)
+        @pl.when(core == 0)
+        def _():
+            pltpu.make_async_copy(x_ref, xr.at[me], x_sem).start()
+            pltpu.make_async_copy(y_part(chip), yr.at[me], y_sem).start()
+
+        @pl.when(core == 1)
+        def _():
+            remote(x_ref, xr.at[me], send_sem.at[2], x_sem, twin).start()
+            remote(y_part(chip), yr.at[me], send_sem.at[3], y_sem, twin).start()
+
+        def one(o):
+            to = (chip + o) % chips
+            remote(x_ref, xr.at[me], send_sem.at[2], x_sem, in_plane(to * CORES)).start()
+            remote(y_part(to), yr.at[me], send_sem.at[3], y_sem, in_plane(to * CORES)).start()
+
+        loop(1, chips, one)
 
     send_raw(0)
-    send_dense()
+    if DENSE_MID:
+        send_dense()
     loop(0, samples, widen(1))
     send_raw(1)
+    if not DENSE_MID:
+        send_dense()
 
     drain(idr, ids_sem)
     rows = lax.broadcasted_iota(jnp.int32, (bs, 128), 0)
@@ -310,16 +329,24 @@
     def rows_at(s):
         return pl.ds(s * sub, sub)
 
-    def send_up(h, t, s):
-        there = up.at[h, t + 1, rows_at(s)]
+    def send_up(h, lane, t, s):
+        there = up.at[h, lane, t + 1, rows_at(s)]
         remote(
-            up.at[h, t, rows_at(s)], there, send_sem.at[4], up_sem.at[h, t + 1, s], along_z((z + 1) % depth)
+            up.at[h, lane, t, rows_at(s)],
+            there,
+            send_sem.at[4],
+            up_sem.at[h, lane, t + 1, s],
+            along_z((z + 1) % depth),
         ).start()
 
-    def send_down(h, t, s):
-        there = down.at[h, t + 1, rows_at(s)]
+    def send_down(h, lane, t, s):
+        there = down.at[h, lane, t + 1, rows_at(s)]
         remote(
-            down.at[h, t, rows_at(s)], there, send_sem.at[5], down_sem.at[h, t + 1, s], along_z((z + depth - 1) % depth)
+            down.at[h, lane, t, rows_at(s)],
+            there,
+            send_sem.at[5],
+            down_sem.at[h, lane, t + 1, s],
+            along_z((z + depth - 1) % depth),
         ).start()
 
     def piece_up(t):
@@ -328,80 +355,146 @@
     def piece_down(t):
         return (z - (half - 1) + t + depth) % depth
 
-    def wait_up(h, t, s):
-        drain(up.at[h, t, rows_at(s)], up_sem.at[h, t, s])
-
-    def wait_down(h, t, s):
-        drain(down.at[h, t, rows_at(s)], down_sem.at[h, t, s])
+    def wait_up(h, lane, t, s):
+        drain(up.at[h, lane, t, rows_at(s)], up_sem.at[h, lane, t, s])
+
+    def wait_down(h, lane, t, s):
+        drain(down.at[h, lane, t, rows_at(s)], down_sem.at[h, lane, t, s])
+
+    def hand_over(h, p):
+        remote(own.at[h, p], given.at[h, p], send_sem.at[12], given_sem.at[h, p], twin).start()
+
+    def feed_all(h):
+        drain(raw.at[h, 0 : plane - 1], raw_sem.at[h])
+        for k in range(shares):
+            product(h, (piece_up(0) // columns + k) % shares)
+            if k == 0:
+                hand_over(h, piece_up(0))
+
+        def one(t):
+            @pl.when(t > 0)
+            def _():
+                hand_over(h, piece_up(t))
+
+            hand_over(h, piece_down(t))
+
+        loop(0, half, one)
+
+    def feed(h):
+        def one(t):
+            product_of(h, piece_up(t))
+            hand_over(h, piece_up(t))
+            product_of(h, piece_down(t))
+            hand_over(h, piece_down(t))
+
+        return one
+
+    def arrive(h, p):
+        drain(given.at[h, p], given_sem.at[h, p])
 
     def begin(h):
         drain(raw.at[h, 0 : plane - 1], raw_sem.at[h])
-        for k in range(shares):
-            if h == 0:
+        if h == 0:
+            for k in range(shares):
                 product(h, (piece_up(0) // columns + k) % shares)
-            elif k == 0:
-                product_of(h, piece_up(0))
-            if k == 0:
-                up[h, 0] = own[h, piece_up(0)]
+        else:
+            product_of(h, piece_up(0))
+            product_of(h, piece_down(0))
+        for lane in (1, 0):
+            source = given if lane == 0 else own
+            if lane == 0:
+                arrive(h, piece_up(0))
+            up[h, lane, 0] = source[h, piece_up(0)]
+            for s in range(SUBS):
+                send_up(h, lane, 0, s)
+            if lane == 0:
+                arrive(h, piece_down(0))
+            down[h, lane, 0] = source[h, piece_down(0)]
+            if half > 1:
                 for s in range(SUBS):
-                    send_up(h, 0, s)
-        if h > 0:
-            product_of(h, piece_down(0))
-        down[h, 0] = own[h, piece_down(0)]
-        if half > 1:
-            for s in range(SUBS):
-                send_down(h, 0, s)
+                    send_down(h, lane, 0, s)
 
     def hop(h, t):
         if h > 0:
             product_of(h, piece_up(t))
             product_of(h, piece_down(t))
+        arrive(h, piece_up(t))
+        arrive(h, piece_down(t))
         for s in range(SUBS):
-            wait_up(h, t, s)
-            up[h, t, rows_at(s)] += own[h, piece_up(t), rows_at(s)]
-            send_up(h, t, s)
-            wait_down(h, t, s)
-            down[h, t, rows_at(s)] += own[h, piece_down(t), rows_at(s)]
-            send_down(h, t, s)
+            for lane in (1, 0):
+                source = given if lane == 0 else own
+                wait_up(h, lane, t, s)
+                up[h, lane, t, rows_at(s)] += source[h, piece_up(t), rows_at(s)]
+                send_up(h, lane, t, s)
+                wait_down(h, lane, t, s)
+                down[h, lane, t, rows_at(s)] += source[h, piece_down(t), rows_at(s)]
+                send_down(h, lane, t, s)
 
     def last(h):
         t = half - 1
         if h > 0:
             product_of(h, piece_up(t))
             product_of(h, z)
+        if half > 1:
+            arrive(h, piece_up(t))
+            arrive(h, z)
         for s in range(SUBS):
-            wait_up(h, t, s)
-            up[h, t, rows_at(s)] += own[h, piece_up(t), rows_at(s)]
-            send_up(h, t, s)
+            for lane in (1, 0):
+                source = given if lane == 0 else own
+                wait_up(h, lane, t, s)
+                up[h, lane, t, rows_at(s)] += source[h, piece_up(t), rows_at(s)]
+                send_up(h, lane, t, s)
         for s in range(SUBS):
-            wait_down(h, t, s)
-            final[h, rows_at(s)] = down[h, t, rows_at(s)] + own[h, z, rows_at(s)]
+            for lane in (1, 0):
+                source = given if lane == 0 else own
+                wait_down(h, lane, t, s)
+                final[h, lane, rows_at(s)] = down[h, lane, t, rows_at(s)] + source[h, z, rows_at(s)]
 
     def finish(h):
-        for s in range(SUBS):
-            wait_up(h, half, s)
-            final[h, rows_at(s)] = (final[h, rows_at(s)] + up[h, half, rows_at(s)]) * (1.0 / 12.0)
-            piece = final.at[h, rows_at(s)]
-            place = table_ref.at[rows_at(s), h * width : (h + 1) * width]
+        for lane in (1, 0):
+            for s in range(SUBS):
+                wait_up(h, lane, half, s)
+            total = (final[h, lane] + up[h, lane, half]) * (1.0 / 12.0)
+            step = jnp.maximum(jnp.max(jnp.abs(total), axis=0, keepdims=True), tiny) * (1.0 / steps_16)
+            scaled = total / step
+            whole = (scaled + jnp.where(scaled >= 0.0, 0.5, -0.5)).astype(jnp.int32)
+            coded[h, lane] = whole.astype(jnp.int16)
+            steps_out[h, lane] = jnp.broadcast_to(step, (8, width))
+            moves = (
+                (coded.at[h, lane], coded_in.at[h], coded_sem.at[h]),
+                (steps_out.at[h, lane], steps_in.at[h], steps_sem.at[h]),
+            )
+
+            def away(device, moves=moves):
+                for k, (src, dst, sem) in enumerate(moves):
+                    remote(src, dst, send_sem.at[10 + k], sem, device).start()
 
             @pl.when(piece_self)
-            def _(piece=piece, place=place):
-                pltpu.make_async_copy(piece, place, table_sem).start()
+            def _(moves=moves, away=away, lane=lane):
+                if lane == 1:
+                    for src, dst, sem in moves:
+                        pltpu.make_async_copy(src, dst, sem).start()
+                else:
+                    away(twin)
 
             @pl.when(jnp.logical_not(piece_self))
-            def _(piece=piece, place=place):
-                remote(piece, place, send_sem.at[10], table_sem, (dp_of(xl, piece_z, core), piece_blk)).start()
-
-    def pass_input():
-        drain(xr.at[core], x_sem.at[0])
-        remote(xr.at[core], xr.at[core], send_sem.at[11], x_sem.at[1], twin).start()
+            def _(away=away, lane=lane):
+                away((dp_of(xl, piece_z, lane), piece_blk))
+
+    def store_table():
+        for h in range(HALVES):
+            drain(coded_in.at[h], coded_sem.at[h])
+            drain(steps_in.at[h], steps_sem.at[h])
+            values = coded_in[h].astype(jnp.int32).astype(F32)
+            table_out[:, h * width : (h + 1) * width] = values * steps_in[h, 0:1, :]
+        pltpu.make_async_copy(table_out, table_ref, table_sem).start()
 
     def dense_one():
+        drain(xr, x_sem)
         drain(yr, y_sem)
-        drain(xr.at[core], x_sem.at[1])
         partial = lax.dot_general(
             xr[...].reshape(kdim, bs),
-            yr[...].reshape(kdim, bs),
+            yr[...].reshape(kdim, wide_bs),
             (((0,), (0,)), ((), ())),
             preferred_element_type=F32,
         )
@@ -423,59 +516,68 @@
 
         loop(1, depth, one)
 
-    def block_place(q):
-        return update_ref.at[:, pl.ds(pl.multiple_of(q * bs, bs), bs)]
+    def chip_place(chip_of):
+        return update_ref.at[:, pl.ds(pl.multiple_of(chip_of * wide_bs, wide_bs), wide_bs)]
+
+    def block_of(b):
+        return grad[...].reshape(bs, wide_bs)[:, b * bs : (b + 1) * bs]
 
     def dense_three():
         drain(grad.at[0 : depth - 1], grad_sem)
         grad[z] = own_sum[...]
-        block = grad[...].reshape(bs, bs)
         for copy in local[2:5]:
             copy.wait()
-        moment = second_beta * moment_in[...] + (1.0 - second_beta) * block * block
-        graft = block / (jnp.sqrt(moment) + graft_epsilon)
-        halfway = jnp.dot(left_root[...], block, precision=highest, preferred_element_type=F32)
-        precond = jnp.dot(halfway, right_root[...], precision=highest, preferred_element_type=F32)
-        ratio = jnp.sqrt(jnp.sum(graft * graft) / (jnp.sum(precond * precond) + norm_epsilon))
-        block_update[...] = (precond * ratio).astype(BF16)
-        place = block_place(me)
+        for b in range(CORES):
+            cut = slice(b * bs, (b + 1) * bs)
+            block = block_of(b)
+            moment = second_beta * moment_in[:, cut] + (1.0 - second_beta) * block * block
+            graft = block / (jnp.sqrt(moment) + graft_epsilon)
+            halfway = jnp.dot(left_root[b], block, precision=highest, preferred_element_type=F32)
+            precond = jnp.dot(halfway, right_root[b], precision=highest, preferred_element_type=F32)
+            ratio = jnp.sqrt(jnp.sum(graft * graft) / (jnp.sum(precond * precond) + norm_epsilon))
+            block_update[:, cut] = (precond * ratio).astype(BF16)
+            mmat[b] = moment
+        place = chip_place(chip)
 
         def one(o):
-            remote(block_update, place, send_sem.at[8], update_sem.at[o], same_core((chip + o) % chips)).start()
+            to = in_plane(((chip + o) % chips) * CORES)
+            remote(block_update, place, send_sem.at[8], update_sem.at[o], to).start()
 
         loop(1, chips, one)
         remote(block_update, place, send_sem.at[8], passed_sem, twin).start()
         pltpu.make_async_copy(block_update, place, update_sem.at[0]).start()
-        mmat[...] = moment
 
     def statistics():
-        block = grad[...].reshape(bs, bs)
-        lmat[...] = lax.dot_general(
-            block, block, (((1,), (1,)), ((), ())), precision=highest, preferred_element_type=F32
-        )
-        rmat[...] = lax.dot_general(
-            block, block, (((0,), (0,)), ((), ())), precision=highest, preferred_element_type=F32
-        )
+        for b in range(CORES):
+            block = block_of(b)
+            lmat[b] = lax.dot_general(
+                block, block, (((1,), (1,)), ((), ())), precision=highest, preferred_element_type=F32
+            )
+            rmat[b] = lax.dot_general(
+                block, block, (((0,), (0,)), ((), ())), precision=highest, preferred_element_type=F32
+            )
         stage[...] = jnp.zeros(stage.shape, F32)
 
-        def rows_for(o):
-            other = (g + o) % GROUP
+        def rows_for(other):
             first = dp_of(other // CORES, z, other % CORES) * share
-            for kind, matrix in enumerate((lmat, rmat, mmat)):
-                for r in range(share):
-                    stage[other, kind, r : r + 1, :] = matrix[pl.ds(first + r, 1), :]
+            for b in range(CORES):
+                for kind, matrix in enumerate((lmat, rmat, mmat)):
+                    for r in range(share):
+                        stage[other, b, kind, r : r + 1, :] = matrix[b, pl.ds(first + r, 1), :]
 
         loop(0, GROUP, rows_for)
+        place = stats.at[pl.ds(xl * CORES, CORES)]
+        pltpu.make_async_copy(stage.at[g], place, stats_sem).start()
 
         def one_group(o):
             other = (g + o) % GROUP
-            remote(stage.at[other], stats.at[g], send_sem.at[9], stats_sem, in_plane(blk * GROUP + other)).start()
+            remote(stage.at[other], place, send_sem.at[9], stats_sem, in_plane(blk * GROUP + other)).start()
 
         loop(1, GROUP, one_group)
 
     def pass_update():
         def one(o):
-            place = block_place(((chip + chips - o) % chips) * CORES + core)
+            place = chip_place((chip + chips - o) % chips)
             pltpu.make_async_copy(place, place, update_sem.at[o]).wait()
             remote(place, place, send_sem.at[8], passed_sem, twin).start()
 
@@ -490,8 +592,7 @@
     def store_statistics():
         local[5].wait()
         local[6].wait()
-        drain(stats.at[0 : GROUP - 1], stats_sem)
-        stats[g] = stage[g]
+        drain(stats, stats_sem)
         for other in range(GROUP):
             left_out[other, 0] = left_stats[other, 0] + stats[other, 0, 0:share, :]
             right_out[other, 0] = right_stats[other, 0] + stats[other, 1, 0:share, :]
@@ -501,43 +602,88 @@
 
     lag = min(LAG, half + 1)
     end = half + lag
-    dense = {}
-    parts_of_dense = (pass_input, dense_one, dense_two, dense_three, statistics, pass_update, store_statistics)
-    for at, part_of in zip(DENSE_AT, parts_of_dense):
-        dense.setdefault(min(at, end), []).append(part_of)
 
     def kind(t):
         return "" if t < 0 or t > half else "b" if t == 0 else "f" if t == half else "l" if t == half - 1 else "h"
 
-    step = 0
-    while step <= end:
-        kinds = (kind(step), kind(step - lag))
-        stop = step + 1
-        while stop <= end and "h" in kinds and (kind(stop), kind(stop - lag)) == kinds and not dense.get(stop - 1):
-            stop += 1
-
-        def run(t, kinds=kinds):
-            for h, what in enumerate(kinds):
-                if what == "b":
-                    begin(h)
-                elif what == "h":
-                    hop(h, t - h * lag)
-                elif what == "l":
-                    last(h)
-                elif what == "f":
-                    finish(h)
-
-        if stop - step > 1:
-            loop(step, stop, run)
-        else:
-            run(step)
-        for part_of in dense.get(stop - 1, ()):
-            part_of()
-        step = stop
-
+    def ring():
+        step = 0
+        while step <= end:
+            kinds = (kind(step), kind(step - lag))
+            stop = step + 1
+            while stop <= end and "h" in kinds and (kind(stop), kind(stop - lag)) == kinds:
+                stop += 1
+
+            def run(t, kinds=kinds):
+                for h, what in enumerate(kinds):
+                    if what == "b":
+                        begin(h)
+                    elif what == "h":
+                        hop(h, t - h * lag)
+                    elif what == "l":
+                        last(h)
+                    elif what == "f":
+                        finish(h)
+
+            if stop - step > 1:
+                loop(step, stop, run)
+            else:
+                run(step)
+            step = stop
+
+    def dense():
+        feed_all(0)
+        if DENSE_MID:
+            dense_one()
+            dense_two()
+        drain(raw.at[1, 0 : plane - 1], raw_sem.at[1])
+        loop(0, half, feed(1))
+        if not DENSE_MID:
+            dense_one()
+            dense_two()
+        dense_three()
+        statistics()
+        pass_update()
+
+    @pl.when(core == 0)
+    def _():
+        dense()
+        drain(xr.at[0 : chips - 1], send_sem.at[2])
+        drain(yr.at[0 : chips - 1], send_sem.at[3])
+        drain(own, send_sem.at[12])
+        drain(parts.at[0 : depth - 1], send_sem.at[6])
+        drain(grad.at[0 : depth - 1], send_sem.at[7])
+        drain(chip_place(chip), update_sem.at[0])
+        for _ in range(CORES):
+            drain(update_ref.at[:, 0 : (chips - 1) * wide_bs], send_sem.at[8])
+        drain(chip_place(0), send_sem.at[8])
+        drain(stage.at[0 : GROUP - 1], send_sem.at[9])
+
+    @pl.when(core == 1)
+    def _():
+        ring()
+        for copy in local[2:5]:
+            copy.wait()
+        drain(update_ref, passed_sem)
+        drain(xr.at[0:chips], send_sem.at[2])
+        drain(yr.at[0:chips], send_sem.at[3])
+        drain(up.at[:, :, 0:half], send_sem.at[4])
+        if half > 1:
+            drain(down.at[:, :, 0 : half - 1], send_sem.at[5])
+
+        @pl.when(jnp.logical_not(piece_self))
+        def _():
+            drain(coded, send_sem.at[10])
+            drain(steps_out, send_sem.at[11])
+
+        @pl.when(piece_self)
+        def _():
+            drain(coded.at[:, 0], send_sem.at[10])
+            drain(steps_out.at[:, 0], send_sem.at[11])
+
+    store_statistics()
+    store_table()
     drain(table_ref, table_sem)
-    drain(block_place(me), update_sem.at[0])
-    drain(update_ref.at[:, 0 : chips * bs], passed_sem)
     for copy in results:
         copy.wait()
 
@@ -551,21 +697,6 @@
 
     for h in range(HALVES):
         drain(raw.at[h, 0 : plane - 1], send_sem.at[1])
-    drain(xr.at[0, 0 : chips - 1], send_sem.at[2])
-    drain(xr.at[0], send_sem.at[11])
-    drain(yr.at[0, 0 : chips - 1], send_sem.at[3])
-    drain(yr.at[0], send_sem.at[3])
-    drain(up.at[:, 0:half], send_sem.at[4])
-    if half > 1:
-        drain(down.at[:, 0 : half - 1], send_sem.at[5])
-    drain(parts.at[0 : depth - 1], send_sem.at[6])
-    drain(grad.at[0 : depth - 1], send_sem.at[7])
-    drain(update_ref.at[:, 0 : (plane - 1) * bs], send_sem.at[8])
-    drain(stats.at[0 : GROUP - 1], send_sem.at[9])
-
-    @pl.when(jnp.logical_not(piece_self))
-    def _():
-        drain(final, send_sem.at[10])
 
 
 def place_kernel(cuts, *refs):
@@ -646,24 +777,30 @@
             vmem((shares, columns * bs, plane * samples), BF16),
             vmem((HALVES, plane, shares, samples, width), BF16),
             vmem((HALVES, depth, bs, width), F32),
-            vmem((HALVES, half + 1, bs, width), F32),
-            vmem((HALVES, half, bs, width), F32),
-            vmem((HALVES, bs, width), F32),
-            vmem((CORES, chips, samples, kdim), BF16),
-            vmem((CORES, chips, samples, bs), BF16),
-            vmem((depth, bs // depth, bs), F32),
-            vmem((depth, bs // depth, bs), F32),
-            vmem((bs // depth, bs), F32),
-            vmem((depth, bs // depth, bs), F32),
-            vmem((bs, bs), F32),
-            vmem((bs, bs), F32),
-            vmem((bs, bs), F32),
+            vmem((HALVES, depth, bs, width), F32),
+            vmem((HALVES, CORES, half + 1, bs, width), F32),
+            vmem((HALVES, CORES, half, bs, width), F32),
+            vmem((HALVES, CORES, bs, width), F32),
+            vmem((HALVES, CORES, bs, width), jnp.int16),
+            vmem((HALVES, CORES, 8, width), F32),
+            vmem((HALVES, bs, width), jnp.int16),
+            vmem((HALVES, 8, width), F32),
+            vmem((bs, edim), F32),
+            vmem((plane, samples, kdim), BF16),
+            vmem((plane, samples, CORES * bs), BF16),
+            vmem((depth, bs // depth, CORES * bs), F32),
+            vmem((depth, bs // depth, CORES * bs), F32),
+            vmem((bs // depth, CORES * bs), F32),
+            vmem((depth, bs // depth, CORES * bs), F32),
+            vmem((CORES, bs, bs), F32),
+            vmem((CORES, bs, bs), F32),
+            vmem((CORES, bs, bs), F32),
+            vmem((GROUP, CORES, 3, 8, bs), F32),
             vmem((GROUP, 3, 8, bs), F32),
-            vmem((GROUP, 3, 8, bs), F32),
-            vmem((bs, bs), BF16),
-            vmem((bs, bs), F32),
-            vmem((bs, bs), F32),
-            vmem((bs, bs), F32),
+            vmem((bs, CORES * bs), BF16),
+            vmem((CORES, bs, bs), F32),
+            vmem((CORES, bs, bs), F32),
+            vmem((bs, CORES * bs), F32),
             vmem(left_stats.shape, F32),
             vmem(right_stats.shape, F32),
             vmem(left_stats.shape, F32),
@@ -674,17 +811,20 @@
             dma((3,)),
             dma,
             dma((HALVES,)),
-            dma((2,)),
             dma,
-            dma((HALVES, half + 1, SUBS)),
-            dma((HALVES, half, SUBS)),
+            dma,
+            dma((HALVES, depth)),
+            dma((HALVES, CORES, half + 1, SUBS)),
+            dma((HALVES, CORES, half, SUBS)),
+            dma((HALVES,)),
+            dma((HALVES,)),
             dma,
             dma,
             dma,
             dma,
             dma((chips,)),
             dma,
-            dma((12,)),
+            dma((13,)),
         ],
         compiler_params=pltpu.CompilerParams(
             collective_id=0, has_side_effects=True, vmem_limit_bytes=56 * 1024 * 1024

time: 108 us -> 99.8 us (0.924); the launches traced: 106 us -> 98.8 us
  Pallas kernels: 105 us -> 98.1 us
    pallas_call x1, Pallas kernels: 103 us -> 96 us  [per_device(): pl.pallas_call(functools.partial(exchange_kernel, depth, columns), out_sh...]
where the time goes in v3:
time: 99.8 us; the launch traced here: 98.8 us
  Pallas kernels  98.1 us (98%)
    pallas_call x1, Pallas kernels, per_device(): pl.pallas_call(functools.partial(exchange_kernel, depth, columns), out_sh...  96 us
    pallas_call x1, Pallas kernels, per_device(): pl.pallas_call(functools.partial(place_kernel, cuts), out_shape=shapes, i...  2.14 us

profile of v3, /device:TPU:24, one launch (start us, length us, event | category | flops | bytes accessed | tf_op | source)
XLA Modules:
  0.0 98.8 jit_solution(10203656448214810889)
XLA Ops:
  0.6 96.0 %exchange.1 = (f32[128,256]{1,0:T(8,128)}, f32[4,1,2,128]{3,2,1,0:T(2,128)}, f32[4,1,2,128]{3,2,1,0:T(2,128)}, f32[1,2,512]{2,1,0:T(2,128)}, bf16[128,4096]{1,0:T(8,128)(2,1)}) custom-call(s32[64]{0:T(128)} %slots_ref.1, bf16[64,64,256]{2,1,0:T(8,128)(2,1)} %pooled_ref.1, s32[64,4,64]{2,1,0:T(4,128)} %bitcast.8, s32[64,64]{1,0:T(8,128)} %bitcast.9, ...), custom_call_target="tpu_custom_call" | custom-call | tf_op jit(solution)/shard_map/exchange/pallas_call | solution.py:764
  96.7 2.1 %place.1 = (f32[128,256]{1,0:T(8,128)}, f32[4,1,2,128]{3,2,1,0:T(2,128)}, f32[4,1,2,128]{3,2,1,0:T(2,128)}, f32[1,2,512]{2,1,0:T(2,128)}, bf16[128,4096]{1,0:T(8,128)(2,1)}) custom-call(f32[128,256]{1,0:T(8,128)} %get-tuple-element.15.refs_0_, f32[4,1,2,128]{3,2,1,0:T(2,128)} %get-tuple-element.16.refs_1_, f32[4,1,2,128]{3,2,1,0:T(2,128)} %get-tuple-element.17.refs_2_, ...), custom_call_target="tpu_custom_call" | custom-call | tf_op jit(solution)/shard_map/place/pallas_call | solution.py:846
